TPU v7x, 256 devices: a whole 4x4x8 slice. The times are simulated.
256 devices in a mesh: lat: 64 (over z_lo, x, y, core), ch: 4 (over z_hi).
Axes of the slice: x: 4, y: 4, z: 8 (z_hi: 4, z_lo: 2; z = z_hi * 2 + z_lo), core: 2. Of those that a mesh axis runs over, the one named last changes fastest.
Arguments:
- x_field: bfloat16 [192, 256, 1440], P('lat', 'ch'), may hold values from -16 to 16
- cotangent: bfloat16 [192, 256, 1440], P('lat', 'ch'), may hold values from -6 to 6
- halo_rows: int32 [192, 5], P('lat'), may hold values from -1 to 191, as said below
- filters: bfloat16 [192, 5, 9, 16], P('lat'), may hold values from -0.625 to 0.625
- mixing: bfloat16 [9, 256, 256], replicated, may hold values from -0.125 to 0.125
Outputs:
- y_field: bfloat16 [192, 256, 1440], P('lat', 'ch')
- x_grad: bfloat16 [192, 256, 1440], P('lat', 'ch')
- w_grad: float32 [256, 9, 256], P('lat', None, 'ch')
Inputs may be any that keep to these rules, and one draw needn't show every extreme that they name: The entries of halo_rows[i] other than -1 are distinct latitudes within 2 of i, and always include i - 1, i and i + 1 where these lie in the grid; their order among the slots is arbitrary.
All inputs are finite; a program needn't handle non-finite values.
Results may differ from a plain program's by a relative error of at most 0.006.
Values may be sent and summed in bfloat16 or wider, within the bound.
No kernel may reach another device: no remote copies, remote signals or barrier semaphores. Data moves between devices by JAX's collectives and lax.ppermute only.
A program may use at most 128 MiB of HBM per device.

v0:
```python
import math

import jax
import jax.numpy as jnp
from jax import lax
from jax.sharding import PartitionSpec as P


def padded_2(cells, sides, width):
    for axis, dim in sides:
        count = lax.axis_size(axis)
        ends = count - 1
        head = lax.slice_in_dim(cells, 0, width, axis=dim)
        tail = lax.slice_in_dim(cells, cells.shape[dim] - width, cells.shape[dim], axis=dim)
        cells = jnp.concatenate(
            [
                lax.ppermute(tail, axis, [(i, (i + 1) % count) for i in range(ends)]),
                cells,
                lax.ppermute(head, axis, [((i + 1) % count, i) for i in range(ends)]),
            ],
            axis=dim,
        )
    return cells


def shifted(value, axis, steps):
    count = lax.axis_size(axis)
    initial, last = (max(0, -steps), min(count, count - steps))
    return lax.ppermute(value, axis, [(source, source + steps) for source in range(initial, last)])


def build_taps(rows_block, filt_block, base, count, nbasis, ntaps):
    hit = (
        rows_block[:, :, None] - base == jnp.arange(count, dtype=jnp.int32)[None, None, :]
    ).astype(jnp.float32)
    taps = jnp.einsum("irs,irkl->iksl", hit, filt_block.astype(jnp.float32))
    return taps.reshape(rows_block.shape[0] * nbasis, count, ntaps).astype(jnp.bfloat16)


def spread(field, taps):
    ntaps = taps.shape[2]
    nlon = field.shape[2]
    front = ntaps // 2
    back = ntaps - 1 - front
    padded = jnp.concatenate([field[:, :, nlon - front :], field, field[:, :, :back]], axis=2)
    return lax.conv_general_dilated(
        padded,
        taps,
        (1,),
        "VALID",
        dimension_numbers=("CNH", "OIH", "CNH"),
        preferred_element_type=jnp.float32,
    )


def collect(grad, taps):
    ntaps = taps.shape[2]
    nlon = grad.shape[2]
    front = ntaps - 1 - ntaps // 2
    back = ntaps // 2
    padded = jnp.concatenate([grad[:, :, nlon - front :], grad, grad[:, :, :back]], axis=2)
    return lax.conv_general_dilated(
        padded,
        taps[:, :, ::-1],
        (1,),
        "VALID",
        dimension_numbers=("CNH", "IOH", "CNH"),
        preferred_element_type=jnp.float32,
    )


def local(x_field, cotangent, halo_rows, filters, mixing):
    rows_dev, own_ch, nlon = x_field.shape
    nbasis = mixing.shape[0]
    width = mixing.shape[1]
    ntaps = filters.shape[3]
    reach = (halo_rows.shape[1] - 1) // 2
    span = rows_dev + 2 * reach
    start = lax.axis_index("lat") * rows_dev
    ch_start = lax.axis_index("ch") * own_ch
    whole = lax.all_gather(x_field, "ch", axis=1, tiled=True)
    window = padded_2(whole, (("lat", 0),), reach)
    taps = build_taps(halo_rows, filters, start - reach, span, nbasis, ntaps)
    basis = spread(window, taps).astype(jnp.bfloat16).reshape(rows_dev, nbasis, width, nlon)
    out_weights = lax.dynamic_slice_in_dim(mixing, ch_start, own_ch, 2)
    y_field = jnp.einsum(
        "ikcj,kco->ioj", basis, out_weights, preferred_element_type=jnp.float32
    ).astype(jnp.bfloat16)
    grad_all = lax.all_gather(cotangent, "ch", axis=1, tiled=True)
    in_weights = lax.dynamic_slice_in_dim(mixing, ch_start, own_ch, 1)
    basis_grad = jnp.einsum(
        "ioj,kco->ikcj", grad_all, in_weights, preferred_element_type=jnp.float32
    ).astype(jnp.bfloat16)
    weight_term = jnp.einsum("ikcj,ioj->cko", basis, cotangent, preferred_element_type=jnp.float32)
    scale = 1.0 / math.sqrt(lax.axis_size("lat") * rows_dev * nlon)
    w_grad = lax.psum_scatter(weight_term, "lat", scatter_dimension=0, tiled=True) * scale
    partial_grad = collect(basis_grad.reshape(rows_dev * nbasis, own_ch, nlon), taps)
    lower_rim = partial_grad[:reach]
    upper_rim = partial_grad[span - reach :]
    from_next = shifted(lower_rim.astype(jnp.bfloat16), "lat", -1).astype(lower_rim.dtype)
    from_prev = shifted(upper_rim, "lat", 1)
    core = partial_grad[reach : reach + rows_dev]
    core = core + jnp.pad(from_prev, ((0, rows_dev - reach), (0, 0), (0, 0)))
    core = core + jnp.pad(from_next, ((rows_dev - reach, 0), (0, 0), (0, 0)))
    x_grad = core.astype(jnp.bfloat16)
    return (y_field, x_grad, w_grad)


def solution(mesh):
    return jax.shard_map(
        local,
        mesh=mesh,
        in_specs=(
            P("lat", "ch", None),
            P("lat", "ch", None),
            P("lat", None),
            P("lat", None, None, None),
            P(),
        ),
        out_specs=(P("lat", "ch", None), P("lat", "ch", None), P("lat", None, "ch")),
        check_vma=False,
    )
```

profile of v0, /device:TPU:1, one launch (start us, length us, event | category | flops | bytes accessed | tf_op | source)
XLA Modules:
  0.0 596.9 jit_solution(18097941911041887081)
XLA Ops:
  7.2 0.0 copy-start
  7.2 0.0 all-gather.5.cloned.1.call-start
  7.2 0.7 all-gather.5.cloned.1.call-update
  7.9 0.0 all-gather.3.cloned.1.call-start
  8.0 0.7 all-gather.3.cloned.1.call-update
  8.7 0.0 reduce-scatter.2.cloned.1.call-start
  8.7 0.7 broadcast_subtract_fusion
  9.4 0.9 convolution_convert_fusion.1
  10.3 0.2 copy.35
  10.5 59.2 %all-gather.5.cloned.1.call-done = bf16[3,256,1440]{2,1,0:T(8,128)(2,1)} async-done(((bf16[3,64,1440]{2,1,0:T(8,128)(2,1)}), bf16[3,256,1440]{2,1,0:T(8,128)(2,1)}) %all-gather.5.cloned.1.call-update) | async-done | bytes 2211856 | tf_op jit(solution)/shard_map/all_gather | solution.py:89
  69.7 3.2 convert_bitcast_fusion
  72.9 0.6 copy.37
  73.5 0.2 slice.39
  73.7 2.1 copy-done.2
  75.8 0.1 slice.40
  75.9 50.0 %all-gather.3.cloned.1.call-done = bf16[3,256,1440]{2,1,0:T(8,128)(2,1)} async-done(((bf16[3,64,1440]{2,1,0:T(8,128)(2,1)}), bf16[3,256,1440]{2,1,0:T(8,128)(2,1)}) %all-gather.3.cloned.1.call-update) | async-done | bytes 2211856 | tf_op jit(solution)/shard_map/all_gather | solution.py:81
  125.9 5.6 copy.31
  131.6 6.8 %fusion.28 = (bf16[2,256,1440]{1,0,2:T(2,128)(2,1)}, bf16[2,256,1440]{1,0,2:T(2,128)(2,1)}) fusion(bf16[3,256,1440]{1,0,2:T(4,128)(2,1)} %copy.31), kind=kLoop, calls=%fused_computation.39 | loop fusion | bytes 5898240 | tf_op jit(solution)/shard_map/slice | solution.py:14
  138.4 2.5 collective-permute-start.1
  140.9 3.2 collective-permute-start
  144.1 10.4 %concatenate.11 = bf16[27,64,1455]{2,1,0:T(8,128)(2,1)} concatenate(bf16[27,64,7]{2,1,0:T(8,128)(2,1)S(1)} %slice.39, bf16[27,64,1440]{2,1,0:T(8,128)(2,1)} %bitcast.51, bf16[27,64,8]{2,1,0:T(8,128)(2,1)S(1)} %slice.40), dimensions={2} | concatenate | bytes 10056960 | tf_op jit(solution)/shard_map/concatenate | solution.py:61
  154.6 18.0 %copy.38 = bf16[27,64,1455]{1,0,2:T(8,128)(2,1)} copy(bf16[27,64,1455]{2,1,0:T(8,128)(2,1)} %concatenate.11) | data formatting | bytes 10056960 | tf_op jit(solution)/shard_map/concatenate | solution.py:61
  172.6 27.3 %fusion.29 = f32[7,64,1440]{1,0,2:T(8,128)S(1)} fusion(bf16[27,64,1455]{1,0,2:T(8,128)(2,1)} %copy.38, bf16[27,7,16]{0,1,2:T(8,128)(2,1)S(1)} %copy.35), kind=kOutput, calls=%fused_computation.40 | convolution fusion | flops 557383680 | bytes 7615008 | tf_op jit(solution)/shard_map/conv_general_dilated | solution.py:62
  199.9 2.5 copy-done.3
  202.5 1.0 slice.42
  203.5 2.3 copy.40
  205.8 2.3 collective-permute-start.2
  208.1 3.0 slice.50
  211.1 0.9 copy.42
  212.0 2.9 collective-permute-start.3
  214.9 6.2 %collective-permute-done.3 = bf16[2,64,1440]{2,1,0:T(8,128)(2,1)S(1)} collective-permute-done((bf16[2,64,1440]{2,1,0:T(8,128)(2,1)S(1)}, bf16[2,64,1440]{2,1,0:T(8,128)(2,1)S(1)}, u32[]{:S(2)}, u32[]{:S(2)}) %collective-permute-start.3) | collective-permute-done | bytes 368672 | tf_op jit(solution)/shard_map/ppermute | solution.py:29
  221.1 0.9 copy.43
  222.1 0.0 collective-permute-done.2
  222.1 2.9 copy.41
  225.0 4.8 fusion.12
  229.8 3.2 copy.45
  233.1 0.0 collective-permute-done.1
  233.1 0.0 collective-permute-done
  233.1 34.4 %convolution_convert_fusion = bf16[27,256,1440]{1,0,2:T(8,128)(2,1)} fusion(bf16[27,7,16]{0,1,2:T(8,128)(2,1)S(1)} %copy.35, bf16[2,256,1440]{1,0,2:T(2,128)(2,1)} %collective-permute-done.1, bf16[3,256,1440]{1,0,2:T(4,128)(2,1)} %copy.31, bf16[2,256,1440]{1,0,2:T(2,128)(2,1)} %collective-permute-done), kind=kOutput, calls=%fused_computation | convolution fusion | flops 2286420480 | bytes 25073568 | tf_op jit(solution)/shard_map/conv_general_dilated | solution.py:46
  267.5 19.0 %copy.36 = bf16[27,256,1440]{1,2,0:T(8,128)(2,1)S(1)} copy(bf16[27,256,1440]{1,0,2:T(8,128)(2,1)} %convolution_convert_fusion) | data formatting | bytes 39813120 | tf_op jit(solution)/shard_map/convert_element_type | solution.py:84
  286.5 6.7 %copy-done.1 = bf16[27,256,1440]{1,2,0:T(8,128)(2,1)} copy-done((bf16[27,256,1440]{1,2,0:T(8,128)(2,1)}, bf16[27,256,1440]{1,2,0:T(8,128)(2,1)S(1)}, u32[]{:S(2)}) %copy-start.1) | copy-done | bytes 19906584
  293.2 3.5 convolution_bitcast_fusion.1
  296.8 2.5 copy.44
  299.3 0.0 reduce-scatter.2.cloned.1.call-update
  299.3 13.6 %fusion.14 = bf16[3,64,1440]{2,1,0:T(8,128)(2,1)} fusion(bf16[3,9,256,1440]{2,3,1,0:T(8,128)(2,1)} %bitcast.48, bf16[9,256,256]{2,1,0:T(8,128)(2,1)S(1)} %copy-done, s32[]{:T(128)S(6)} %select_n.4), kind=kOutput, calls=%fused_computation.20 | convolution fusion | flops 1274296320 | bytes 21049348 | tf_op jit(solution)/shard_map/ikcj,kco->ioj/dot_general | solution.py:86
  312.9 275.6 %reduce-scatter.2.cloned.1.call-done = f32[4,9,64]{2,1,0:T(8,128)} async-done(((f32[256,9,64]{2,1,0:T(8,128)}), f32[4,9,64]{2,1,0:T(8,128)}) %reduce-scatter.2.cloned.1.call-update) | async-done | bytes 9232 | tf_op jit(solution)/shard_map/reduce_scatter | solution.py:96
  588.5 0.8 broadcast_multiply_fusion
  589.3 0.6 copy.46
  (6 shorter events, 0.0 us)
Async XLA Ops:
  7.2 62.5 %copy-start = (bf16[9,256,256]{2,1,0:T(8,128)(2,1)S(1)}, bf16[9,256,256]{2,1,0:T(8,128)(2,1)}, u32[]{:S(2)}) copy-start(bf16[9,256,256]{2,1,0:T(8,128)(2,1)} %param.9) | copy-start | bytes 3538948
  7.2 62.5 %all-gather.5.cloned.1.call-start = ((), (), s32[]{:S(2)}) async-start(), calls=%async_computation.2 | async-start | bytes 2949120 | tf_op jit(solution)/shard_map/all_gather | solution.py:89
  7.9 118.0 %all-gather.3.cloned.1.call-start = ((), (), s32[]{:S(2)}) async-start(), calls=%async_computation.1 | async-start | bytes 2949120 | tf_op jit(solution)/shard_map/all_gather | solution.py:81
  8.7 579.9 %reduce-scatter.2.cloned.1.call-start = ((), (), s32[]{:S(2)}) async-start(), calls=%async_computation.3 | async-start | bytes 2129920 | tf_op jit(solution)/shard_map/reduce_scatter | solution.py:96
  73.5 2.3 copy-start.2
  138.4 94.7 %collective-permute-start.1 = (bf16[2,256,1440]{1,0,2:T(2,128)(2,1)}, bf16[2,256,1440]{1,0,2:T(2,128)(2,1)}, u32[]{:S(2)}, u32[]{:S(2)}) collective-permute-start(bf16[2,256,1440]{1,0,2:T(2,128)(2,1)} %get-tuple-element.13), channel_id=1, source_target_pairs={{4,0},{8,4},{12,8},{16,12},{20,16},{24,20},{28,24},{32,28},{36,32}... | collective-permute-start | bytes 4423688 | tf_op jit(solution)/shard_map/ppermute | solution.py:19
  140.9 92.2 %collective-permute-start = (bf16[2,256,1440]{1,0,2:T(2,128)(2,1)}, bf16[2,256,1440]{1,0,2:T(2,128)(2,1)}, u32[]{:S(2)}, u32[]{:S(2)}) collective-permute-start(bf16[2,256,1440]{1,0,2:T(2,128)(2,1)} %get-tuple-element.12), channel_id=1, source_target_pairs={{0,4},{4,8},{8,12},{12,16},{16,20},{20,24},{24,28},{28,32},{32,36}... | collective-permute-start | bytes 4423688 | tf_op jit(solution)/shard_map/ppermute | solution.py:17
  199.9 2.5 copy-start.3
  205.8 16.3 %collective-permute-start.2 = (f32[2,64,1440]{2,1,0:T(8,128)}, f32[2,64,1440]{2,1,0:T(8,128)}, u32[]{:S(2)}, u32[]{:S(2)}) collective-permute-start(f32[2,64,1440]{2,1,0:T(8,128)} %copy.40), channel_id=1, source_target_pairs={{0,4},{4,8},{8,12},{12,16},{16,20},{20,24},{24,28},{28,32},{32,36}... | collective-permute-start | bytes 2211848 | tf_op jit(solution)/shard_map/ppermute | solution.py:29
  212.0 9.1 %collective-permute-start.3 = (bf16[2,64,1440]{2,1,0:T(8,128)(2,1)S(1)}, bf16[2,64,1440]{2,1,0:T(8,128)(2,1)S(1)}, u32[]{:S(2)}, u32[]{:S(2)}) collective-permute-start(bf16[2,64,1440]{2,1,0:T(8,128)(2,1)S(1)} %copy.42), channel_id=1, source_target_pairs={{4,0},{8,4},{12,8},{16,12},{20,16},{24,20},{28,24},{32,28},{36,32}... | collective-permute-start | bytes 1105928 | tf_op jit(solution)/shard_map/ppermute | solution.py:29
  267.5 25.7 %copy-start.4 = (bf16[3,64,1440]{2,1,0:T(8,128)(2,1)S(1)}, bf16[3,64,1440]{2,1,0:T(8,128)(2,1)}, u32[]{:S(2)}) copy-start(bf16[3,64,1440]{2,1,0:T(8,128)(2,1)} %param.6) | copy-start | bytes 1658884
  286.5 6.7 %copy-start.1 = (bf16[27,256,1440]{1,2,0:T(8,128)(2,1)}, bf16[27,256,1440]{1,2,0:T(8,128)(2,1)S(1)}, u32[]{:S(2)}) copy-start(bf16[27,256,1440]{1,2,0:T(8,128)(2,1)S(1)} %copy.36) | copy-start | bytes 59719684
Sparse Core Ops, SparseCore 0:
  9.8 59.8 all-gather.4
  71.5 54.3 all-gather.2
  299.4 289.0 reduce-scatter.1
where the time goes:
time: 605 us; the launch traced here: 597 us
  waiting for transfers between devices  392 us (65%)
  local copies, waits for them, and re-layouts  89.7 us (15%)
  matrix products  83 us (14%)
  between operations  14.4 us (2%)
  starting transfers between devices  11 us (2%)
  other arithmetic  6.3 us (1%)
    reduce_scatter x1, waiting for transfers between devices, local(): lax.psum_scatter(weight_term, 'lat', scatter_dimension=0, tiled=True)  276 us
    all_gather x1, waiting for transfers between devices, local(): grad_all = lax.all_gather(cotangent, 'ch', axis=1, tiled=True)  59.2 us
    all_gather x1, waiting for transfers between devices, local(): whole = lax.all_gather(x_field, 'ch', axis=1, tiled=True)  50 us
    conv_general_dilated x1, matrix products, spread(): lax.conv_general_dilated(padded, taps, (1,), 'VALID', dimension_numbers=(...  34.4 us
    concatenate x2, local copies, waits for them, and re-layouts, collect(): jnp.concatenate([grad[:, :, nlon - front:], grad, grad[:, :, :back]], axi...  28.5 us
    conv_general_dilated x1, matrix products, collect(): lax.conv_general_dilated(padded, taps[:, :, ::-1], (1,), 'VALID', dimensi...  27.3 us
    convert_element_type x1, local copies, waits for them, and re-layouts, local(): spread(window, taps).astype(jnp.bfloat16)  19 us
    unnamed x12, local copies, waits for them, and re-layouts  15.3 us
  transfers between devices with their start and end apart: 7, of which 4 were waited for; matrix products, arithmetic and copies ran while one was open for 16% of the time, Pallas kernels for 0%

commit v1 on v0

v1 whole, which is shorter than its diff:
```python
import functools
import math

import jax
import jax.numpy as jnp
from jax import lax
from jax.experimental import pallas as pl
from jax.experimental.pallas import tpu as pltpu
from jax.sharding import PartitionSpec as P

BF = jnp.bfloat16
F32 = jnp.float32
ROWS = 3
OWN = 64
C = 256
J = 1440
K = 9
PART = 360
WIN = 384
PAD = 400
BLK = 32
SPAN = 48
REACH = 2
NSP = 5
X_OFF = 16
G_OFF = 8
VMEM_LIMIT = 56 * 1024 * 1024

VM = pl.BlockSpec(memory_space=pltpu.VMEM)
SM = pl.BlockSpec(memory_space=pltpu.SMEM)


def call(body, name, outs, n_in, scratch=(), flops=0, nbytes=0):
    return pl.pallas_call(
        body,
        out_shape=[jax.ShapeDtypeStruct(s, d) for s, d in outs],
        in_specs=[SM] + [VM] * n_in,
        out_specs=[VM] * len(outs),
        scratch_shapes=list(scratch),
        compiler_params=pltpu.CompilerParams(vmem_limit_bytes=VMEM_LIMIT),
        cost_estimate=pl.CostEstimate(flops=flops, bytes_accessed=nbytes, transcendentals=0),
        name=name,
    )


def pick4(value):
    return lax.rem(value + 4, 4)


def pack_body(off, idx, x, o0, o1, o2, o3, win):
    ch = idx[0]
    for r in range(ROWS):
        v = x[r]
        for h in range(4):
            a = PART * h - off
            if a < 0:
                w = jnp.concatenate([v[:, J + a :], v[:, : WIN + a]], axis=1)
            elif a + WIN > J:
                w = jnp.concatenate([v[:, a:], v[:, : a + WIN - J]], axis=1)
            else:
                w = v[:, a : a + WIN]
            win[h, r] = w
    for s, o in enumerate((o0, o1, o2, o3)):
        o[...] = win[pick4(ch + s)]


def gather_parts(ch, refs, scr):
    for s, ref in enumerate(refs):
        src = pick4(ch - s)
        scr[:, pl.ds(pl.multiple_of(src * OWN, OWN), OWN), :] = ref[...]


def asm_x_body(idx, p0, p1, p2, p3, out, head, tail, scr):
    gather_parts(idx[0], (p0, p1, p2, p3), scr)
    zeros = jnp.zeros((PAD - WIN, C), BF)
    for r in range(ROWS):
        t = scr[r].T
        for dst, pos in ((out, r), (head, r), (tail, r - 1)):
            if 0 <= pos < dst.shape[0]:
                dst[pos, :WIN, :] = t
                dst[pos, WIN:, :] = zeros


def asm_g_body(idx, p0, p1, p2, p3, out, out_t, scr):
    gather_parts(idx[0], (p0, p1, p2, p3), scr)
    lane = lax.broadcasted_iota(jnp.int32, (C, WIN), 1)
    own = (lane >= G_OFF) & (lane < G_OFF + PART)
    for r in range(ROWS):
        v = scr[r]
        out[r] = v.T
        out_t[r] = jnp.where(own, v.astype(F32), 0.0).astype(BF)


def bands_body(idx, a, b, ta, tb):
    for n in range(ROWS * K):
        i, k = divmod(n, K)
        row = jnp.broadcast_to(a[n : n + 1, :], (BLK, 256))
        ta[i, k * BLK : (k + 1) * BLK, :] = pltpu.roll(row, 0, 1, stride=1, stride_axis=0).astype(BF)
    for n in range(ROWS * NSP):
        i, sp = divmod(n, NSP)
        row = jnp.broadcast_to(b[n : n + 1, :], (BLK, 512))
        tb[i, sp * BLK : (sp + 1) * BLK, :] = pltpu.roll(row, 0, 1, stride=1, stride_axis=0).astype(BF)


def forward_body(idx, x, xp, xn, ta, gt, mix, y0, y1, y2, y3, keep, send, basis, yt):
    ch = idx[0]
    core = idx[1]
    rows = [xp.at[0], xp.at[1], x.at[0], x.at[1], x.at[2], xn.at[0], xn.at[1]]
    zeros = jnp.zeros((256 - NSP * SPAN, C), BF)

    @pl.loop(0, WIN // BLK)
    def _(b):
        at = pl.multiple_of(b * BLK, BLK)
        for i in range(ROWS):
            rhs = jnp.concatenate([rows[i + sp][pl.ds(at, SPAN), :] for sp in range(NSP)] + [zeros], axis=0)
            out = jnp.dot(ta[i], rhs, preferred_element_type=F32).astype(BF)
            for k in range(K):
                basis[pl.ds(pl.multiple_of(i * WIN + at, BLK), BLK), k * C : (k + 1) * C] = out[k * BLK : (k + 1) * BLK]

    m = mix[...]
    for i in range(ROWS):
        y = jnp.dot(basis[i * WIN : (i + 1) * WIN, :], m, preferred_element_type=F32)
        yt[i] = y.T.astype(BF)
    for s, o in enumerate((y0, y1, y2, y3)):
        o[...] = yt[:, pl.ds(pl.multiple_of(pick4(ch + s) * OWN, OWN), OWN), :]

    g = jnp.concatenate([gt[i] for i in range(ROWS)], axis=1)
    low = lax.broadcasted_iota(jnp.int32, (16, 8, C), 1) < 4
    first = core == 0
    for k in range(K):
        w = jnp.dot(g, basis[:, k * C : (k + 1) * C], preferred_element_type=F32).T
        t = w.reshape(2, 16, 8, C)
        even = jnp.where(low, t[0], pltpu.roll(t[1], 4, 1))
        odd = jnp.where(low, pltpu.roll(t[0], 4, 1), t[1])
        keep[:, 8 * k : 8 * k + 8, :] = jnp.where(first, even, odd)
        send[:, 8 * k : 8 * k + 8, :] = jnp.where(first, odd, even)


def backward_body(idx, g, tb, mix, mid, lower, upper, bg):
    bg[:, WIN:, :] = jnp.zeros((ROWS, PAD - WIN, K * C), BF)
    for i in range(ROWS):
        for k in range(K):
            bg[i, :WIN, k * C : (k + 1) * C] = lax.dot_general(
                g[i], mix[k * C : (k + 1) * C, :], (((1,), (1,)), ((), ())), preferred_element_type=F32
            ).astype(BF)
    zeros = jnp.zeros((512 - K * SPAN, C), BF)

    @pl.loop(0, WIN // BLK)
    def _(b):
        at = pl.multiple_of(b * BLK, BLK)
        acc = [None] * (ROWS + 2 * REACH)
        for i in range(ROWS):
            rhs = jnp.concatenate(
                [bg[i, pl.ds(at, SPAN), k * C : (k + 1) * C] for k in range(K)] + [zeros], axis=0
            )
            out = jnp.dot(tb[i], rhs, preferred_element_type=F32)
            for sp in range(NSP):
                part = out[sp * BLK : (sp + 1) * BLK]
                acc[i + sp] = part if acc[i + sp] is None else acc[i + sp] + part
        for n in range(2):
            lower[n, pl.ds(at, BLK), :] = acc[n].astype(BF)
            upper[n, pl.ds(at, BLK), :] = acc[ROWS + REACH + n].astype(BF)
        for n in range(ROWS):
            mid[n, pl.ds(at, BLK), :] = acc[REACH + n]


def join_body(idx, mid, prev, after, o0, o1, o2, o3, scr):
    ch = idx[0]
    for r in range(ROWS):
        v = mid[r]
        if r < REACH:
            v = v + prev[r].astype(F32)
        if r >= ROWS - REACH:
            v = v + after[r - (ROWS - REACH)].astype(F32)
        scr[r] = v.T.astype(BF)
    for s, o in enumerate((o0, o1, o2, o3)):
        o[...] = scr[:, pl.ds(pl.multiple_of(pick4(ch + s) * OWN, OWN), OWN), :]


def unpack_body(off, idx, p0, p1, p2, p3, out, scr):
    for s, ref in enumerate((p0, p1, p2, p3)):
        scr[pick4(idx[0] - s)] = ref[...]
    for r in range(ROWS):
        out[r] = jnp.concatenate([scr[h, r][:, off : off + PART] for h in range(4)], axis=1)


def fold_y_body(idx, keep, got, own, o1, o2, o3):
    for s, o in enumerate((own, o1, o2, o3)):
        t = pick4(idx[2] + s)
        for x in range(4):
            v = keep[x * 4 + t] + got[x * 4 + t]
            o[x * 72 : (x + 1) * 72, :] = v.astype(o.dtype)


def fold_x_body(idx, own, r1, r2, r3, o0, o1, o2, o3, scr):
    total = own[...] + r1[...].astype(F32) + r2[...].astype(F32) + r3[...].astype(F32)
    scr[...] = total.reshape(4, 72, C)
    for s, o in enumerate((o0, o1, o2, o3)):
        o[...] = scr[pick4(idx[3] + s)]


def fold_ch_body(idx, own, r1, r2, r3, o0, o1, o2, o3, scr):
    total = own[...] + r1[...] + r2[...] + r3[...]
    for h in range(4):
        scr[h] = total[:, h * OWN : (h + 1) * OWN]
    for s, o in enumerate((o0, o1, o2, o3)):
        o[...] = scr[pick4(idx[0] + s)]


def fold_z_body(idx, own, r1, r2, r3, out):
    out[...] = own[...] + r1[...] + r2[...] + r3[...]


def ring_ch(step):
    return [(i, (i + step) % 4) for i in range(4)]


def ring_lat(place, step):
    out = []
    for i in range(64):
        digit = i // place % 4
        out.append((i, i + ((digit + step) % 4 - digit) * place))
    return out


def local(x_field, cotangent, halo_rows, filters, mixing):
    lat = lax.axis_index("lat")
    ch = lax.axis_index("ch")
    idx = jnp.stack([ch, lat % 2, lat // 2 % 4, lat // 8 % 4]).astype(jnp.int32)
    mix2 = mixing.reshape(K * C, C)
    part = ((ROWS, OWN, WIN), BF)

    def exchange(parts):
        return [parts[0]] + [lax.ppermute(parts[s], "ch", ring_ch(s)) for s in (1, 2, 3)]

    def packed(value, off, name):
        return call(
            functools.partial(pack_body, off), name, [part] * 4, 1, [pltpu.VMEM((4, ROWS, OWN, WIN), BF)]
        )(idx, value)

    x_parts = exchange(packed(x_field, X_OFF, "pack_x"))
    g_parts = exchange(packed(cotangent, G_OFF, "pack_g"))

    want = lat * ROWS + jnp.arange(ROWS, dtype=jnp.int32)[:, None] - REACH + jnp.arange(NSP, dtype=jnp.int32)[None, :]
    hit = (halo_rows[:, :, None] == want[:, None, :]) & (halo_rows[:, :, None] >= 0)
    taps = jnp.sum(jnp.where(hit[:, :, None, :, None], filters.astype(F32)[:, :, :, None, :], 0.0), axis=1)
    ntap = taps.shape[-1]
    a = jnp.pad(taps, ((0, 0),) * 3 + ((0, SPAN - ntap),)).reshape(ROWS * K, NSP * SPAN)
    a = jnp.pad(a, ((0, 0), (0, 256 - NSP * SPAN)))
    b = jnp.pad(taps[..., ::-1], ((0, 0),) * 3 + ((1, SPAN - ntap - 1),))
    b = jnp.transpose(b, (0, 2, 1, 3)).reshape(ROWS * NSP, K * SPAN)
    b = jnp.pad(b, ((0, 0), (0, 512 - K * SPAN)))
    ta, tb = call(
        bands_body, "bands", [((ROWS, K * BLK, 256), BF), ((ROWS, NSP * BLK, 512), BF)], 2
    )(idx, a, b)

    lon = (ROWS, PAD, C)
    rim = (REACH, PAD, C)
    x_lon, x_head, x_tail = call(
        asm_x_body, "asm_x", [(lon, BF), (rim, BF), (rim, BF)], 4, [pltpu.VMEM((ROWS, C, WIN), BF)]
    )(idx, *x_parts)
    up = [(i, i + 1) for i in range(63)]
    down = [(i + 1, i) for i in range(63)]
    x_prev = lax.ppermute(x_tail, "lat", up)
    x_next = lax.ppermute(x_head, "lat", down)

    g_lon, g_t = call(
        asm_g_body,
        "asm_g",
        [((ROWS, WIN, C), BF), ((ROWS, C, WIN), BF)],
        4,
        [pltpu.VMEM((ROWS, C, WIN), BF)],
    )(idx, *g_parts)

    *y_parts, keep, send = call(
        forward_body,
        "forward",
        [part] * 4 + [((16, 72, C), F32)] * 2,
        6,
        [pltpu.VMEM((ROWS * WIN, K * C), BF), pltpu.VMEM((ROWS, C, WIN), BF)],
        flops=6_000_000_000,
        nbytes=8_000_000,
    )(idx, x_lon, x_prev, x_next, ta, g_t, mix2)
    got = lax.ppermute(send, "lat", [(i, i ^ 1) for i in range(64)])
    y_parts = exchange(y_parts)

    mid, lower, upper = call(
        backward_body,
        "backward",
        [((ROWS, WIN, C), F32), ((REACH, WIN, C), BF), ((REACH, WIN, C), BF)],
        3,
        [pltpu.VMEM((ROWS, PAD, K * C), BF)],
        flops=4_000_000_000,
        nbytes=8_000_000,
    )(idx, g_lon, tb, mix2)
    from_prev = lax.ppermute(upper, "lat", up)
    from_next = lax.ppermute(lower, "lat", down)

    own, s1, s2, s3 = call(
        fold_y_body, "fold_y", [((288, C), F32)] + [((288, C), BF)] * 3, 2
    )(idx, keep, got)
    r = [lax.ppermute(v, "lat", ring_lat(2, s)) for s, v in ((1, s1), (2, s2), (3, s3))]
    own, s1, s2, s3 = call(
        fold_x_body, "fold_x", [((72, C), F32)] * 4, 4, [pltpu.VMEM((4, 72, C), F32)]
    )(idx, own, *r)
    r = [lax.ppermute(v, "lat", ring_lat(8, s)) for s, v in ((1, s1), (2, s2), (3, s3))]
    own, s1, s2, s3 = call(
        fold_ch_body, "fold_ch", [((72, OWN), F32)] * 4, 4, [pltpu.VMEM((4, 72, OWN), F32)]
    )(idx, own, *r)
    r = [lax.ppermute(v, "ch", ring_ch(s)) for s, v in ((1, s1), (2, s2), (3, s3))]
    (half,) = call(fold_z_body, "fold_z", [((72, OWN), F32)], 4)(idx, own, *r)
    other = lax.ppermute(half, "lat", [(i, i ^ 32) for i in range(64)])
    both = ((half + other) * (1.0 / math.sqrt(64 * ROWS * J))).reshape(K, 2, 4, OWN)
    w_grad = jnp.transpose(lax.dynamic_index_in_dim(both, lat // 32, 1, keepdims=False), (1, 0, 2))

    g_out = call(join_body, "join", [part] * 4, 3, [pltpu.VMEM((ROWS, C, WIN), BF)])(
        idx, mid, from_prev, from_next
    )
    g_out = exchange(g_out)

    def unpacked(parts, off, name):
        (out,) = call(
            functools.partial(unpack_body, off),
            name,
            [((ROWS, OWN, J), BF)],
            4,
            [pltpu.VMEM((4, ROWS, OWN, WIN), BF)],
        )(idx, *parts)
        return out

    y_field = unpacked(y_parts, G_OFF, "unpack_y")
    x_grad = unpacked(g_out, 0, "unpack_g")
    return (y_field, x_grad, w_grad)


def solution(mesh):
    return jax.shard_map(
        local,
        mesh=mesh,
        in_specs=(
            P("lat", "ch", None),
            P("lat", "ch", None),
            P("lat", None),
            P("lat", None, None, None),
            P(),
        ),
        out_specs=(P("lat", "ch", None), P("lat", "ch", None), P("lat", None, "ch")),
        check_vma=False,
    )
```

time: 605 us -> 147 us (0.24); the launches traced: 597 us -> 147 us
  waiting for transfers between devices: 392 us -> 31 us
  matrix products: 83 us -> 0 us
  local copies, waits for them, and re-layouts: 89.7 us -> 9.32 us
  starting transfers between devices: 11 us -> 60.2 us
  Pallas kernels: 0 us -> 44.5 us
  between operations: 14.4 us -> 0.99 us
    reduce_scatter x1 -> x0, waiting for transfers between devices: 276 us -> none  [local(): lax.psum_scatter(weight_term, 'lat', scatter_dimension=0, tiled=True)]
    all_gather x2 -> x0, waiting for transfers between devices: 109 us -> none  [the longest x1 59.2 us: local(): grad_all = lax.all_gather(cotangent, 'ch', axis=1, tiled=True)]
    conv_general_dilated x2 -> x0, matrix products: 61.7 us -> none  [the longest x1 34.4 us: spread(): lax.conv_general_dilated(padded, taps, (1,), 'VALID', dimension_numbers=(...]
    ppermute x4 -> x27, starting transfers between devices: 10.9 us -> 60.2 us  [the longest x12 28.9 us: exchange(): lax.ppermute(parts[s], 'ch', ring_ch(s))]
    pallas_call x0 -> x14, Pallas kernels: none -> 44.5 us  [the longest x1 10.2 us: local(): call(forward_body, 'forward', [part] * 4 + [((16, 72, C), F32)] * 2, 6, [...]
    concatenate x2 -> x0, local copies, waits for them, and re-layouts: 28.5 us -> none  [collect(): jnp.concatenate([grad[:, :, nlon - front:], grad, grad[:, :, :back]], axi...]
    ppermute x4 -> x27, waiting for transfers between devices: 6.22 us -> 31 us  [the longest x12 22.9 us: exchange(): lax.ppermute(parts[s], 'ch', ring_ch(s))]
    dot_general x4 -> x0, matrix products: 21.3 us -> none  [the longest x1 13.6 us: local(): jnp.einsum('ikcj,kco->ioj', basis, out_weights, preferred_element_type=jn...]
  transfers between devices with their start and end apart: 7 -> 27, of which waited for: 4 -> 10; matrix products, arithmetic and copies ran while one was open for 16% -> 1% of each run, Pallas kernels for 0% -> 22%
where the time goes in v1:
time: 147 us
  starting transfers between devices  60.2 us (41%)
  Pallas kernels  44.5 us (30%)
  waiting for transfers between devices  31 us (21%)
  local copies, waits for them, and re-layouts  9.32 us (6%)
    ppermute x12, starting transfers between devices, exchange(): lax.ppermute(parts[s], 'ch', ring_ch(s))  28.9 us
    ppermute x12, waiting for transfers between devices, exchange(): lax.ppermute(parts[s], 'ch', ring_ch(s))  22.9 us
    pallas_call x1, Pallas kernels, local(): call(forward_body, 'forward', [part] * 4 + [((16, 72, C), F32)] * 2, 6, [...  10.2 us
    pallas_call x1, Pallas kernels, local(): call(backward_body, 'backward', [((ROWS, WIN, C), F32), ((REACH, WIN, C),...  7.93 us
    ppermute x3, starting transfers between devices, local(): lax.ppermute(v, 'ch', ring_ch(s))  7.1 us
    unnamed x66, local copies, waits for them, and re-layouts  6.89 us
    ppermute x3, starting transfers between devices, local(): lax.ppermute(v, 'lat', ring_lat(8, s))  6.52 us
    ppermute x3, starting transfers between devices, local(): lax.ppermute(v, 'lat', ring_lat(2, s))  6.38 us
  transfers between devices with their start and end apart: 27, of which 10 were waited for; matrix products, arithmetic and copies ran while one was open for 1% of the time, Pallas kernels for 22%

profile of v1, /device:TPU:1, one launch (start us, length us, event | category | flops | bytes accessed | tf_op | source)
XLA Modules:
  0.0 146.8 jit_solution(3660234175372352494)
XLA Ops:
  1.3 2.2 %pack_x.1 = (bf16[3,64,384]{2,1,0:T(8,128)(2,1)}, bf16[3,64,384]{2,1,0:T(8,128)(2,1)}, bf16[3,64,384]{2,1,0:T(8,128)(2,1)}, bf16[3,64,384]{2,1,0:T(8,128)(2,1)}) custom-call(s32[4]{0:T(128)} %pad_add_fusion.idx, bf16[3,64,1440]{2,1,0:T(8,128)(2,1)} %x.10), custom_call_target="tpu_custom_call" | custom-call | tf_op jit(solution)/shard_map/pack_x/pallas_call | solution.py:237
  3.5 3.8 %collective-permute-start = (bf16[3,64,384]{2,1,0:T(8,128)(2,1)}, bf16[3,64,384]{2,1,0:T(8,128)(2,1)S(1)}, u32[]{:S(2)}, u32[]{:S(2)}) collective-permute-start(bf16[3,64,384]{2,1,0:T(8,128)(2,1)} %get-tuple-element.44), channel_id=1, source_target_pairs={{0,1},{1,2},{2,3},{3,0},{4,5},{5,6},{6,7},{7,4},{8,9},{9,10},{10,1... | collective-permute-start | bytes 442376 | tf_op jit(solution)/shard_map/ppermute | solution.py:234
  7.4 5.1 %collective-permute-start.1 = (bf16[3,64,384]{2,1,0:T(8,128)(2,1)}, bf16[3,64,384]{2,1,0:T(8,128)(2,1)S(1)}, u32[]{:S(2)}, u32[]{:S(2)}) collective-permute-start(bf16[3,64,384]{2,1,0:T(8,128)(2,1)} %get-tuple-element.45), channel_id=1, source_target_pairs={{0,2},{1,3},{2,0},{3,1},{4,6},{5,7},{6,4},{7,5},{8,10},{9,11},{10,... | collective-permute-start | bytes 442376 | tf_op jit(solution)/shard_map/ppermute | solution.py:234
  12.5 2.4 %collective-permute-start.2 = (bf16[3,64,384]{2,1,0:T(8,128)(2,1)}, bf16[3,64,384]{2,1,0:T(8,128)(2,1)S(1)}, u32[]{:S(2)}, u32[]{:S(2)}) collective-permute-start(bf16[3,64,384]{2,1,0:T(8,128)(2,1)} %get-tuple-element.46), channel_id=1, source_target_pairs={{0,3},{1,0},{2,1},{3,2},{4,7},{5,4},{6,5},{7,6},{8,11},{9,8},{10,9... | collective-permute-start | bytes 442376 | tf_op jit(solution)/shard_map/ppermute | solution.py:234
  14.9 2.3 %pack_g.1 = (bf16[3,64,384]{2,1,0:T(8,128)(2,1)}, bf16[3,64,384]{2,1,0:T(8,128)(2,1)}, bf16[3,64,384]{2,1,0:T(8,128)(2,1)}, bf16[3,64,384]{2,1,0:T(8,128)(2,1)}) custom-call(s32[4]{0:T(128)} %pad_add_fusion.idx, bf16[3,64,1440]{2,1,0:T(8,128)(2,1)} %x.11), custom_call_target="tpu_custom_call" | custom-call | tf_op jit(solution)/shard_map/pack_g/pallas_call | solution.py:237
  17.1 2.1 %collective-permute-start.6 = (bf16[3,64,384]{2,1,0:T(8,128)(2,1)}, bf16[3,64,384]{2,1,0:T(8,128)(2,1)S(1)}, u32[]{:S(2)}, u32[]{:S(2)}) collective-permute-start(bf16[3,64,384]{2,1,0:T(8,128)(2,1)} %get-tuple-element.53), channel_id=1, source_target_pairs={{0,2},{1,3},{2,0},{3,1},{4,6},{5,7},{6,4},{7,5},{8,10},{9,11},{10,... | collective-permute-start | bytes 442376 | tf_op jit(solution)/shard_map/ppermute | solution.py:234
  19.5 2.5 %collective-permute-start.7 = (bf16[3,64,384]{2,1,0:T(8,128)(2,1)}, bf16[3,64,384]{2,1,0:T(8,128)(2,1)S(1)}, u32[]{:S(2)}, u32[]{:S(2)}) collective-permute-start(bf16[3,64,384]{2,1,0:T(8,128)(2,1)} %get-tuple-element.54), channel_id=1, source_target_pairs={{0,3},{1,0},{2,1},{3,2},{4,7},{5,4},{6,5},{7,6},{8,11},{9,8},{10,9... | collective-permute-start | bytes 442376 | tf_op jit(solution)/shard_map/ppermute | solution.py:234
  22.4 14.1 %collective-permute-done.2.p3 = bf16[3,64,384]{2,1,0:T(8,128)(2,1)S(1)} collective-permute-done((bf16[3,64,384]{2,1,0:T(8,128)(2,1)}, bf16[3,64,384]{2,1,0:T(8,128)(2,1)S(1)}, u32[]{:S(2)}, u32[]{:S(2)}) %collective-permute-start.2) | collective-permute-done | bytes 147488 | tf_op jit(solution)/shard_map/ppermute | solution.py:234
  36.4 0.7 copy-done.18
  37.1 2.5 %asm_x.1 = (bf16[3,400,256]{2,1,0:T(8,128)(2,1)}, bf16[2,400,256]{2,1,0:T(8,128)(2,1)}, bf16[2,400,256]{2,1,0:T(8,128)(2,1)}) custom-call(s32[4]{0:T(128)} %pad_add_fusion.idx, bf16[3,64,384]{2,1,0:T(8,128)(2,1)} %get-tuple-element.43.p0, bf16[3,64,384]{2,1,0:T(8,128)(2,1)} %copy-done.16, bf16[3,64,384]{2,1,0:T(8,128)(2,1)} %copy-done.17, ...), custom_call_target="tpu_custom_call" | custom-call | tf_op jit(solution)/shard_map/asm_x/pallas_call | solution.py:259
  39.6 3.7 %collective-permute-start.3 = (bf16[2,400,256]{2,1,0:T(8,128)(2,1)}, bf16[2,400,256]{2,1,0:T(8,128)(2,1)S(1)}, u32[]{:S(2)}, u32[]{:S(2)}) collective-permute-start(bf16[2,400,256]{2,1,0:T(8,128)(2,1)} %get-tuple-element.48), channel_id=1, source_target_pairs={{0,4},{4,8},{8,12},{12,16},{16,20},{20,24},{24,28},{28,32},{32,36}... | collective-permute-start | bytes 1228808 | tf_op jit(solution)/shard_map/ppermute | solution.py:264
  43.3 1.9 %collective-permute-start.4 = (bf16[2,400,256]{2,1,0:T(8,128)(2,1)}, bf16[2,400,256]{2,1,0:T(8,128)(2,1)S(1)}, u32[]{:S(2)}, u32[]{:S(2)}) collective-permute-start(bf16[2,400,256]{2,1,0:T(8,128)(2,1)} %get-tuple-element.49), channel_id=1, source_target_pairs={{4,0},{8,4},{12,8},{16,12},{20,16},{24,20},{28,24},{32,28},{36,32}... | collective-permute-start | bytes 1228808 | tf_op jit(solution)/shard_map/ppermute | solution.py:265
  46.6 0.6 pad.19.b
  47.2 2.0 %bands.1 = (bf16[3,288,256]{2,1,0:T(8,128)(2,1)}, bf16[3,160,512]{2,1,0:T(8,128)(2,1)}) custom-call(s32[4]{0:T(128)} %pad_add_fusion.idx, f32[27,256]{1,0:T(8,128)} %pad.17.a, f32[15,512]{1,0:T(8,128)} %pad.19.b), custom_call_target="tpu_custom_call" | custom-call | tf_op jit(solution)/shard_map/bands/pallas_call | solution.py:253
  49.9 2.4 %asm_g.1 = (bf16[3,384,256]{2,1,0:T(8,128)(2,1)}, bf16[3,256,384]{2,1,0:T(8,128)(2,1)}) custom-call(s32[4]{0:T(128)} %pad_add_fusion.idx, bf16[3,64,384]{2,1,0:T(8,128)(2,1)} %get-tuple-element.51.p0, bf16[3,64,384]{2,1,0:T(8,128)(2,1)} %copy-done.8, bf16[3,64,384]{2,1,0:T(8,128)(2,1)} %copy-done.9, bf16[3,64,384]{2,1,0:T(8,128)(2,1)} %copy-done.15), custom_call_target="tpu_custom_call" | custom-call | tf_op jit(solution)/shard_map/asm_g/pallas_call | solution.py:267
  53.5 10.2 %forward.1 = (bf16[3,64,384]{2,1,0:T(8,128)(2,1)}, bf16[3,64,384]{2,1,0:T(8,128)(2,1)}, bf16[3,64,384]{2,1,0:T(8,128)(2,1)}, bf16[3,64,384]{2,1,0:T(8,128)(2,1)}...) custom-call(s32[4]{0:T(128)} %pad_add_fusion.idx, bf16[3,400,256]{2,1,0:T(8,128)(2,1)} %get-tuple-element.47.x, ...), custom_call_target="tpu_custom_call" | custom-call | flops 6000000000 | bytes 8000000 | tf_op jit(solution)/shard_map/forward/pallas_call | solution.py:275
  63.7 7.9 %backward.1 = (f32[3,384,256]{2,1,0:T(8,128)}, bf16[2,384,256]{2,1,0:T(8,128)(2,1)}, bf16[2,384,256]{2,1,0:T(8,128)(2,1)}) custom-call(s32[4]{0:T(128)} %pad_add_fusion.idx, bf16[3,384,256]{2,1,0:T(8,128)(2,1)} %get-tuple-element.60.g, bf16[3,160,512]{2,1,0:T(8,128)(2,1)} %get-tuple-element.61.tb, bf16[2304,256]{1,0:T(8,128)(2,1)} %bitcast.14), custom_call_target="tpu_custom_call" | custom-call | flops 4000000000 | bytes 8000000 | tf_op jit(solution)/shard_map/backward/pallas_call | solution.py:287
  71.6 3.6 %collective-permute-start.11 = (bf16[2,384,256]{2,1,0:T(8,128)(2,1)}, bf16[2,384,256]{2,1,0:T(8,128)(2,1)S(1)}, u32[]{:S(2)}, u32[]{:S(2)}) collective-permute-start(bf16[2,384,256]{2,1,0:T(8,128)(2,1)} %get-tuple-element.63), channel_id=1, source_target_pairs={{0,4},{4,8},{8,12},{12,16},{16,20},{20,24},{24,28},{28,32},{32,36}... | collective-permute-start | bytes 1179656 | tf_op jit(solution)/shard_map/ppermute | solution.py:296
  75.2 2.1 %collective-permute-start.12 = (bf16[2,384,256]{2,1,0:T(8,128)(2,1)}, bf16[2,384,256]{2,1,0:T(8,128)(2,1)S(1)}, u32[]{:S(2)}, u32[]{:S(2)}) collective-permute-start(bf16[2,384,256]{2,1,0:T(8,128)(2,1)} %get-tuple-element.64), channel_id=1, source_target_pairs={{4,0},{8,4},{12,8},{16,12},{20,16},{24,20},{28,24},{32,28},{36,32}... | collective-permute-start | bytes 1179656 | tf_op jit(solution)/shard_map/ppermute | solution.py:297
  77.4 1.0 copy-done
  78.4 2.6 %fold_y.1 = (f32[288,256]{1,0:T(8,128)}, bf16[288,256]{1,0:T(8,128)(2,1)}, bf16[288,256]{1,0:T(8,128)(2,1)}, bf16[288,256]{1,0:T(8,128)(2,1)}) custom-call(s32[4]{0:T(128)} %pad_add_fusion.idx, f32[16,72,256]{2,1,0:T(8,128)} %get-tuple-element.69.keep, f32[16,72,256]{2,1,0:T(8,128)} %copy-done), custom_call_target="tpu_custom_call" | custom-call | tf_op jit(solution)/shard_map/fold_y/pallas_call | solution.py:299
  81.0 1.0 collective-permute-start.17
  82.0 4.3 %collective-permute-start.18 = (bf16[288,256]{1,0:T(8,128)(2,1)}, bf16[288,256]{1,0:T(8,128)(2,1)S(1)}, u32[]{:S(2)}, u32[]{:S(2)}) collective-permute-start(bf16[288,256]{1,0:T(8,128)(2,1)} %get-tuple-element.73), channel_id=1, source_target_pairs={{0,16},{4,20},{8,24},{12,28},{16,0},{20,4},{24,8},{28,12},{32,48},... | collective-permute-start | bytes 442376 | tf_op jit(solution)/shard_map/ppermute | solution.py:302
  86.4 1.0 collective-permute-start.19
  87.4 0.7 copy-done.1
  88.3 2.7 %join.1 = (bf16[3,64,384]{2,1,0:T(8,128)(2,1)}, bf16[3,64,384]{2,1,0:T(8,128)(2,1)}, bf16[3,64,384]{2,1,0:T(8,128)(2,1)}, bf16[3,64,384]{2,1,0:T(8,128)(2,1)}) custom-call(s32[4]{0:T(128)} %pad_add_fusion.idx, f32[3,384,256]{2,1,0:T(8,128)} %get-tuple-element.62.mid, bf16[2,384,256]{2,1,0:T(8,128)(2,1)} %copy-done.1, bf16[2,384,256]{2,1,0:T(8,128)(2,1)} %copy-done.2), custom_call_target="tpu_custom_call" | custom-call | tf_op jit(solution)/shard_map/join/pallas_call | solution.py:316
  91.0 1.8 %collective-permute-start.13 = (bf16[3,64,384]{2,1,0:T(8,128)(2,1)}, bf16[3,64,384]{2,1,0:T(8,128)(2,1)S(1)}, u32[]{:S(2)}, u32[]{:S(2)}) collective-permute-start(bf16[3,64,384]{2,1,0:T(8,128)(2,1)} %get-tuple-element.66), channel_id=1, source_target_pairs={{0,1},{1,2},{2,3},{3,0},{4,5},{5,6},{6,7},{7,4},{8,9},{9,10},{10,1... | collective-permute-start | bytes 442376 | tf_op jit(solution)/shard_map/ppermute | solution.py:234
  92.9 1.2 collective-permute-done.19.r3
  94.1 0.7 copy-done.5
  94.7 2.0 %fold_x.1 = (f32[72,256]{1,0:T(8,128)}, f32[72,256]{1,0:T(8,128)}, f32[72,256]{1,0:T(8,128)}, f32[72,256]{1,0:T(8,128)}) custom-call(s32[4]{0:T(128)} %pad_add_fusion.idx, f32[288,256]{1,0:T(8,128)} %get-tuple-element.71.own, bf16[288,256]{1,0:T(8,128)(2,1)} %copy-done.3, bf16[288,256]{1,0:T(8,128)(2,1)} %copy-done.4, bf16[288,256]{1,0:T(8,128)(2,1)} %copy-done.5), custom_call_target="tpu_custom_call" | custom-call | tf_op jit(solution)/shard_map/fold_x/pallas_call | solution.py:303
  96.7 0.8 collective-permute-start.20
  97.5 5.7 %collective-permute-start.21 = (f32[72,256]{1,0:T(8,128)}, f32[72,256]{1,0:T(8,128)S(1)}, u32[]{:S(2)}, u32[]{:S(2)}) collective-permute-start(f32[72,256]{1,0:T(8,128)} %get-tuple-element.77), channel_id=1, source_target_pairs={{0,64},{4,68},{8,72},{12,76},{16,80},{20,84},{24,88},{28,92},{32,9... | collective-permute-start | bytes 221192 | tf_op jit(solution)/shard_map/ppermute | solution.py:306
  103.3 1.2 collective-permute-done.20.r1
  104.5 2.1 %collective-permute-done.21.r2 = f32[72,256]{1,0:T(8,128)S(1)} collective-permute-done((f32[72,256]{1,0:T(8,128)}, f32[72,256]{1,0:T(8,128)S(1)}, u32[]{:S(2)}, u32[]{:S(2)}) %collective-permute-start.21) | collective-permute-done | bytes 73760 | tf_op jit(solution)/shard_map/ppermute | solution.py:306
  107.6 1.8 %fold_ch.1 = (f32[72,64]{1,0:T(8,128)}, f32[72,64]{1,0:T(8,128)}, f32[72,64]{1,0:T(8,128)}, f32[72,64]{1,0:T(8,128)}) custom-call(s32[4]{0:T(128)} %pad_add_fusion.idx, f32[72,256]{1,0:T(8,128)} %get-tuple-element.75.own, f32[72,256]{1,0:T(8,128)} %copy-done.19, f32[72,256]{1,0:T(8,128)} %copy-done.20, f32[72,256]{1,0:T(8,128)} %copy-done.21), custom_call_target="tpu_custom_call" | custom-call | tf_op jit(solution)/shard_map/fold_ch/pallas_call | solution.py:307
  109.4 0.9 collective-permute-start.23
  110.3 4.5 %collective-permute-start.24 = (f32[72,64]{1,0:T(8,128)}, f32[72,64]{1,0:T(8,128)S(1)}, u32[]{:S(2)}, u32[]{:S(2)}) collective-permute-start(f32[72,64]{1,0:T(8,128)} %get-tuple-element.81), channel_id=1, source_target_pairs={{0,2},{1,3},{2,0},{3,1},{4,6},{5,7},{6,4},{7,5},{8,10},{9,11},{10,... | collective-permute-start | bytes 55304 | tf_op jit(solution)/shard_map/ppermute | solution.py:310
  114.8 1.7 %collective-permute-start.25 = (f32[72,64]{1,0:T(8,128)}, f32[72,64]{1,0:T(8,128)S(1)}, u32[]{:S(2)}, u32[]{:S(2)}) collective-permute-start(f32[72,64]{1,0:T(8,128)} %get-tuple-element.82), channel_id=1, source_target_pairs={{0,3},{1,0},{2,1},{3,2},{4,7},{5,4},{6,5},{7,6},{8,11},{9,8},{10,9... | collective-permute-start | bytes 55304 | tf_op jit(solution)/shard_map/ppermute | solution.py:310
  116.5 1.8 %collective-permute-start.14 = (bf16[3,64,384]{2,1,0:T(8,128)(2,1)}, bf16[3,64,384]{2,1,0:T(8,128)(2,1)S(1)}, u32[]{:S(2)}, u32[]{:S(2)}) collective-permute-start(bf16[3,64,384]{2,1,0:T(8,128)(2,1)} %get-tuple-element.67), channel_id=1, source_target_pairs={{0,2},{1,3},{2,0},{3,1},{4,6},{5,7},{6,4},{7,5},{8,10},{9,11},{10,... | collective-permute-start | bytes 442376 | tf_op jit(solution)/shard_map/ppermute | solution.py:234
  118.3 2.1 %collective-permute-start.15 = (bf16[3,64,384]{2,1,0:T(8,128)(2,1)}, bf16[3,64,384]{2,1,0:T(8,128)(2,1)S(1)}, u32[]{:S(2)}, u32[]{:S(2)}) collective-permute-start(bf16[3,64,384]{2,1,0:T(8,128)(2,1)} %get-tuple-element.68), channel_id=1, source_target_pairs={{0,3},{1,0},{2,1},{3,2},{4,7},{5,4},{6,5},{7,6},{8,11},{9,8},{10,9... | collective-permute-start | bytes 442376 | tf_op jit(solution)/shard_map/ppermute | solution.py:234
  120.8 3.6 %collective-permute-start.9 = (bf16[3,64,384]{2,1,0:T(8,128)(2,1)S(1)}, bf16[3,64,384]{2,1,0:T(8,128)(2,1)S(1)}, u32[]{:S(2)}, u32[]{:S(2)}) collective-permute-start(bf16[3,64,384]{2,1,0:T(8,128)(2,1)S(1)} %copy-done.30), channel_id=1, source_target_pairs={{0,2},{1,3},{2,0},{3,1},{4,6},{5,7},{6,4},{7,5},{8,10},{9,11},{10,... | collective-permute-start | bytes 442376 | tf_op jit(solution)/shard_map/ppermute | solution.py:234
  124.4 2.7 %collective-permute-done.25.r3 = f32[72,64]{1,0:T(8,128)S(1)} collective-permute-done((f32[72,64]{1,0:T(8,128)}, f32[72,64]{1,0:T(8,128)S(1)}, u32[]{:S(2)}, u32[]{:S(2)}) %collective-permute-start.25) | collective-permute-done | bytes 18464 | tf_op jit(solution)/shard_map/ppermute | solution.py:310
  127.1 3.3 %collective-permute-start.10 = (bf16[3,64,384]{2,1,0:T(8,128)(2,1)S(1)}, bf16[3,64,384]{2,1,0:T(8,128)(2,1)S(1)}, u32[]{:S(2)}, u32[]{:S(2)}) collective-permute-start(bf16[3,64,384]{2,1,0:T(8,128)(2,1)S(1)} %copy-done.29), channel_id=1, source_target_pairs={{0,3},{1,0},{2,1},{3,2},{4,7},{5,4},{6,5},{7,6},{8,11},{9,8},{10,9... | collective-permute-start | bytes 442376 | tf_op jit(solution)/shard_map/ppermute | solution.py:234
  130.4 1.5 fold_z.1
  131.9 8.2 %collective-permute-done.15.p3 = bf16[3,64,384]{2,1,0:T(8,128)(2,1)S(1)} collective-permute-done((bf16[3,64,384]{2,1,0:T(8,128)(2,1)}, bf16[3,64,384]{2,1,0:T(8,128)(2,1)S(1)}, u32[]{:S(2)}, u32[]{:S(2)}) %collective-permute-start.15) | collective-permute-done | bytes 147488 | tf_op jit(solution)/shard_map/ppermute | solution.py:234
  140.1 0.7 copy-done.13
  140.8 2.2 %unpack_g.1 = bf16[3,64,1440]{2,1,0:T(8,128)(2,1)} custom-call(s32[4]{0:T(128)} %pad_add_fusion.idx, bf16[3,64,384]{2,1,0:T(8,128)(2,1)} %get-tuple-element.65.p0, bf16[3,64,384]{2,1,0:T(8,128)(2,1)} %copy-done.7, bf16[3,64,384]{2,1,0:T(8,128)(2,1)} %copy-done.11, bf16[3,64,384]{2,1,0:T(8,128)(2,1)} %copy-done.13), custom_call_target="tpu_custom_call" | custom-call | tf_op jit(solution)/shard_map/unpack_g/pallas_call | solution.py:322
  143.9 2.2 %unpack_y.1 = bf16[3,64,1440]{2,1,0:T(8,128)(2,1)} custom-call(s32[4]{0:T(128)} %pad_add_fusion.idx, bf16[3,64,384]{2,1,0:T(8,128)(2,1)} %get-tuple-element.56.p0, bf16[3,64,384]{2,1,0:T(8,128)(2,1)} %copy-done.10, bf16[3,64,384]{2,1,0:T(8,128)(2,1)} %copy-done.12, bf16[3,64,384]{2,1,0:T(8,128)(2,1)} %copy-done.14), custom_call_target="tpu_custom_call" | custom-call | tf_op jit(solution)/shard_map/unpack_y/pallas_call | solution.py:322
  (104 shorter events, 7.6 us)
Async XLA Ops:
  0.6 18.6 %copy-start.26 = (s32[3,5]{1,0:T(4,128)S(1)}, s32[3,5]{1,0:T(4,128)}, u32[]{:S(2)}) copy-start(s32[3,5]{1,0:T(4,128)} %param.7) | copy-start | bytes 184
  0.6 18.8 %copy-start.22 = (bf16[3,5,9,16]{3,0,2,1:T(4,128)(2,1)S(1)}, bf16[3,5,9,16]{3,0,2,1:T(4,128)(2,1)}, u32[]{:S(2)}) copy-start(bf16[3,5,9,16]{3,0,2,1:T(4,128)(2,1)} %param.8) | copy-start | bytes 12964
  3.5 15.9 %collective-permute-start = (bf16[3,64,384]{2,1,0:T(8,128)(2,1)}, bf16[3,64,384]{2,1,0:T(8,128)(2,1)S(1)}, u32[]{:S(2)}, u32[]{:S(2)}) collective-permute-start(bf16[3,64,384]{2,1,0:T(8,128)(2,1)} %get-tuple-element.44), channel_id=1, source_target_pairs={{0,1},{1,2},{2,3},{3,0},{4,5},{5,6},{6,7},{7,4},{8,9},{9,10},{10,1... | collective-permute-start | bytes 442376 | tf_op jit(solution)/shard_map/ppermute | solution.py:234
  7.4 15.0 %collective-permute-start.1 = (bf16[3,64,384]{2,1,0:T(8,128)(2,1)}, bf16[3,64,384]{2,1,0:T(8,128)(2,1)S(1)}, u32[]{:S(2)}, u32[]{:S(2)}) collective-permute-start(bf16[3,64,384]{2,1,0:T(8,128)(2,1)} %get-tuple-element.45), channel_id=1, source_target_pairs={{0,2},{1,3},{2,0},{3,1},{4,6},{5,7},{6,4},{7,5},{8,10},{9,11},{10,... | collective-permute-start | bytes 442376 | tf_op jit(solution)/shard_map/ppermute | solution.py:234
  12.5 23.9 %collective-permute-start.2 = (bf16[3,64,384]{2,1,0:T(8,128)(2,1)}, bf16[3,64,384]{2,1,0:T(8,128)(2,1)S(1)}, u32[]{:S(2)}, u32[]{:S(2)}) collective-permute-start(bf16[3,64,384]{2,1,0:T(8,128)(2,1)} %get-tuple-element.46), channel_id=1, source_target_pairs={{0,3},{1,0},{2,1},{3,2},{4,7},{5,4},{6,5},{7,6},{8,11},{9,8},{10,9... | collective-permute-start | bytes 442376 | tf_op jit(solution)/shard_map/ppermute | solution.py:234
  17.1 32.0 %collective-permute-start.5 = (bf16[3,64,384]{2,1,0:T(8,128)(2,1)}, bf16[3,64,384]{2,1,0:T(8,128)(2,1)S(1)}, u32[]{:S(2)}, u32[]{:S(2)}) collective-permute-start(bf16[3,64,384]{2,1,0:T(8,128)(2,1)} %get-tuple-element.52), channel_id=1, source_target_pairs={{0,1},{1,2},{2,3},{3,0},{4,5},{5,6},{6,7},{7,4},{8,9},{9,10},{10,1... | collective-permute-start | bytes 442376 | tf_op jit(solution)/shard_map/ppermute | solution.py:234
  17.1 32.0 %collective-permute-start.6 = (bf16[3,64,384]{2,1,0:T(8,128)(2,1)}, bf16[3,64,384]{2,1,0:T(8,128)(2,1)S(1)}, u32[]{:S(2)}, u32[]{:S(2)}) collective-permute-start(bf16[3,64,384]{2,1,0:T(8,128)(2,1)} %get-tuple-element.53), channel_id=1, source_target_pairs={{0,2},{1,3},{2,0},{3,1},{4,6},{5,7},{6,4},{7,5},{8,10},{9,11},{10,... | collective-permute-start | bytes 442376 | tf_op jit(solution)/shard_map/ppermute | solution.py:234
  19.5 17.0 %copy-start.16 = (bf16[3,64,384]{2,1,0:T(8,128)(2,1)}, bf16[3,64,384]{2,1,0:T(8,128)(2,1)S(1)}, u32[]{:S(2)}) copy-start(bf16[3,64,384]{2,1,0:T(8,128)(2,1)S(1)} %collective-permute-done.p1) | copy-start | bytes 442372
  19.5 29.7 %collective-permute-start.7 = (bf16[3,64,384]{2,1,0:T(8,128)(2,1)}, bf16[3,64,384]{2,1,0:T(8,128)(2,1)S(1)}, u32[]{:S(2)}, u32[]{:S(2)}) collective-permute-start(bf16[3,64,384]{2,1,0:T(8,128)(2,1)} %get-tuple-element.54), channel_id=1, source_target_pairs={{0,3},{1,0},{2,1},{3,2},{4,7},{5,4},{6,5},{7,6},{8,11},{9,8},{10,9... | collective-permute-start | bytes 442376 | tf_op jit(solution)/shard_map/ppermute | solution.py:234
  22.4 14.1 %copy-start.17 = (bf16[3,64,384]{2,1,0:T(8,128)(2,1)}, bf16[3,64,384]{2,1,0:T(8,128)(2,1)S(1)}, u32[]{:S(2)}) copy-start(bf16[3,64,384]{2,1,0:T(8,128)(2,1)S(1)} %collective-permute-done.1.p2) | copy-start | bytes 442372
  39.6 12.7 %collective-permute-start.3 = (bf16[2,400,256]{2,1,0:T(8,128)(2,1)}, bf16[2,400,256]{2,1,0:T(8,128)(2,1)S(1)}, u32[]{:S(2)}, u32[]{:S(2)}) collective-permute-start(bf16[2,400,256]{2,1,0:T(8,128)(2,1)} %get-tuple-element.48), channel_id=1, source_target_pairs={{0,4},{4,8},{8,12},{12,16},{16,20},{20,24},{24,28},{28,32},{32,36}... | collective-permute-start | bytes 1228808 | tf_op jit(solution)/shard_map/ppermute | solution.py:264
  43.3 9.5 %collective-permute-start.4 = (bf16[2,400,256]{2,1,0:T(8,128)(2,1)}, bf16[2,400,256]{2,1,0:T(8,128)(2,1)S(1)}, u32[]{:S(2)}, u32[]{:S(2)}) collective-permute-start(bf16[2,400,256]{2,1,0:T(8,128)(2,1)} %get-tuple-element.49), channel_id=1, source_target_pairs={{4,0},{8,4},{12,8},{16,12},{20,16},{24,20},{28,24},{32,28},{36,32}... | collective-permute-start | bytes 1228808 | tf_op jit(solution)/shard_map/ppermute | solution.py:265
  49.2 0.8 copy-start.15
  52.3 0.8 copy-start.27
  52.7 0.8 copy-start.28
  63.7 13.6 %collective-permute-start.16 = (f32[16,72,256]{2,1,0:T(8,128)}, f32[16,72,256]{2,1,0:T(8,128)S(1)}, u32[]{:S(2)}, u32[]{:S(2)}) collective-permute-start(f32[16,72,256]{2,1,0:T(8,128)} %get-tuple-element.70), channel_id=1, source_target_pairs={{0,4},{4,0},{8,12},{12,8},{16,20},{20,16},{24,28},{28,24},{32,36},... | collective-permute-start | bytes 3538952 | tf_op jit(solution)/shard_map/ppermute | solution.py:284
  71.6 15.7 %collective-permute-start.11 = (bf16[2,384,256]{2,1,0:T(8,128)(2,1)}, bf16[2,384,256]{2,1,0:T(8,128)(2,1)S(1)}, u32[]{:S(2)}, u32[]{:S(2)}) collective-permute-start(bf16[2,384,256]{2,1,0:T(8,128)(2,1)} %get-tuple-element.63), channel_id=1, source_target_pairs={{0,4},{4,8},{8,12},{12,16},{16,20},{20,24},{24,28},{28,32},{32,36}... | collective-permute-start | bytes 1179656 | tf_op jit(solution)/shard_map/ppermute | solution.py:296
  75.2 12.2 %collective-permute-start.12 = (bf16[2,384,256]{2,1,0:T(8,128)(2,1)}, bf16[2,384,256]{2,1,0:T(8,128)(2,1)S(1)}, u32[]{:S(2)}, u32[]{:S(2)}) collective-permute-start(bf16[2,384,256]{2,1,0:T(8,128)(2,1)} %get-tuple-element.64), channel_id=1, source_target_pairs={{4,0},{8,4},{12,8},{16,12},{20,16},{24,20},{28,24},{32,28},{36,32}... | collective-permute-start | bytes 1179656 | tf_op jit(solution)/shard_map/ppermute | solution.py:297
  77.4 1.0 copy-start
  81.0 11.8 %collective-permute-start.17 = (bf16[288,256]{1,0:T(8,128)(2,1)}, bf16[288,256]{1,0:T(8,128)(2,1)S(1)}, u32[]{:S(2)}, u32[]{:S(2)}) collective-permute-start(bf16[288,256]{1,0:T(8,128)(2,1)} %get-tuple-element.72), channel_id=1, source_target_pairs={{0,8},{4,12},{8,16},{12,20},{16,24},{20,28},{24,0},{28,4},{32,40},... | collective-permute-start | bytes 442376 | tf_op jit(solution)/shard_map/ppermute | solution.py:302
  82.0 10.8 %collective-permute-start.18 = (bf16[288,256]{1,0:T(8,128)(2,1)}, bf16[288,256]{1,0:T(8,128)(2,1)S(1)}, u32[]{:S(2)}, u32[]{:S(2)}) collective-permute-start(bf16[288,256]{1,0:T(8,128)(2,1)} %get-tuple-element.73), channel_id=1, source_target_pairs={{0,16},{4,20},{8,24},{12,28},{16,0},{20,4},{24,8},{28,12},{32,48},... | collective-permute-start | bytes 442376 | tf_op jit(solution)/shard_map/ppermute | solution.py:302
  86.4 7.7 %collective-permute-start.19 = (bf16[288,256]{1,0:T(8,128)(2,1)}, bf16[288,256]{1,0:T(8,128)(2,1)S(1)}, u32[]{:S(2)}, u32[]{:S(2)}) collective-permute-start(bf16[288,256]{1,0:T(8,128)(2,1)} %get-tuple-element.74), channel_id=1, source_target_pairs={{0,24},{4,28},{8,0},{12,4},{16,8},{20,12},{24,16},{28,20},{32,56},... | collective-permute-start | bytes 442376 | tf_op jit(solution)/shard_map/ppermute | solution.py:302
  87.4 0.9 copy-start.2
  88.3 32.2 %copy-start.31 = (bf16[3,64,384]{2,1,0:T(8,128)(2,1)S(1)}, bf16[3,64,384]{2,1,0:T(8,128)(2,1)}, u32[]{:S(2)}) copy-start(bf16[3,64,384]{2,1,0:T(8,128)(2,1)} %get-tuple-element.57) | copy-start | bytes 442372
  88.3 32.5 %copy-start.30 = (bf16[3,64,384]{2,1,0:T(8,128)(2,1)S(1)}, bf16[3,64,384]{2,1,0:T(8,128)(2,1)}, u32[]{:S(2)}) copy-start(bf16[3,64,384]{2,1,0:T(8,128)(2,1)} %get-tuple-element.58) | copy-start | bytes 442372
  88.3 38.9 %copy-start.29 = (bf16[3,64,384]{2,1,0:T(8,128)(2,1)S(1)}, bf16[3,64,384]{2,1,0:T(8,128)(2,1)}, u32[]{:S(2)}) copy-start(bf16[3,64,384]{2,1,0:T(8,128)(2,1)} %get-tuple-element.59) | copy-start | bytes 442372
  91.0 27.3 %collective-permute-start.13 = (bf16[3,64,384]{2,1,0:T(8,128)(2,1)}, bf16[3,64,384]{2,1,0:T(8,128)(2,1)S(1)}, u32[]{:S(2)}, u32[]{:S(2)}) collective-permute-start(bf16[3,64,384]{2,1,0:T(8,128)(2,1)} %get-tuple-element.66), channel_id=1, source_target_pairs={{0,1},{1,2},{2,3},{3,0},{4,5},{5,6},{6,7},{7,4},{8,9},{9,10},{10,1... | collective-permute-start | bytes 442376 | tf_op jit(solution)/shard_map/ppermute | solution.py:234
  92.9 1.2 copy-start.3
  92.9 1.2 copy-start.4
  96.7 7.8 %collective-permute-start.20 = (f32[72,256]{1,0:T(8,128)}, f32[72,256]{1,0:T(8,128)S(1)}, u32[]{:S(2)}, u32[]{:S(2)}) collective-permute-start(f32[72,256]{1,0:T(8,128)} %get-tuple-element.76), channel_id=1, source_target_pairs={{0,32},{4,36},{8,40},{12,44},{16,48},{20,52},{24,56},{28,60},{32,6... | collective-permute-start | bytes 221192 | tf_op jit(solution)/shard_map/ppermute | solution.py:306
  97.5 9.1 %collective-permute-start.21 = (f32[72,256]{1,0:T(8,128)}, f32[72,256]{1,0:T(8,128)S(1)}, u32[]{:S(2)}, u32[]{:S(2)}) collective-permute-start(f32[72,256]{1,0:T(8,128)} %get-tuple-element.77), channel_id=1, source_target_pairs={{0,64},{4,68},{8,72},{12,76},{16,80},{20,84},{24,88},{28,92},{32,9... | collective-permute-start | bytes 221192 | tf_op jit(solution)/shard_map/ppermute | solution.py:306
  103.2 3.7 %collective-permute-start.22 = (f32[72,256]{1,0:T(8,128)}, f32[72,256]{1,0:T(8,128)S(1)}, u32[]{:S(2)}, u32[]{:S(2)}) collective-permute-start(f32[72,256]{1,0:T(8,128)} %get-tuple-element.78), channel_id=1, source_target_pairs={{0,96},{4,100},{8,104},{12,108},{16,112},{20,116},{24,120},{28,124... | collective-permute-start | bytes 221192 | tf_op jit(solution)/shard_map/ppermute | solution.py:306
  104.5 2.5 %copy-start.19 = (f32[72,256]{1,0:T(8,128)}, f32[72,256]{1,0:T(8,128)S(1)}, u32[]{:S(2)}) copy-start(f32[72,256]{1,0:T(8,128)S(1)} %collective-permute-done.20.r1) | copy-start | bytes 221188
  109.4 11.1 %collective-permute-start.23 = (f32[72,64]{1,0:T(8,128)}, f32[72,64]{1,0:T(8,128)S(1)}, u32[]{:S(2)}, u32[]{:S(2)}) collective-permute-start(f32[72,64]{1,0:T(8,128)} %get-tuple-element.80), channel_id=1, source_target_pairs={{0,1},{1,2},{2,3},{3,0},{4,5},{5,6},{6,7},{7,4},{8,9},{9,10},{10,1... | collective-permute-start | bytes 55304 | tf_op jit(solution)/shard_map/ppermute | solution.py:310
  110.3 10.5 %collective-permute-start.24 = (f32[72,64]{1,0:T(8,128)}, f32[72,64]{1,0:T(8,128)S(1)}, u32[]{:S(2)}, u32[]{:S(2)}) collective-permute-start(f32[72,64]{1,0:T(8,128)} %get-tuple-element.81), channel_id=1, source_target_pairs={{0,2},{1,3},{2,0},{3,1},{4,6},{5,7},{6,4},{7,5},{8,10},{9,11},{10,... | collective-permute-start | bytes 55304 | tf_op jit(solution)/shard_map/ppermute | solution.py:310
  114.8 12.3 %collective-permute-start.25 = (f32[72,64]{1,0:T(8,128)}, f32[72,64]{1,0:T(8,128)S(1)}, u32[]{:S(2)}, u32[]{:S(2)}) collective-permute-start(f32[72,64]{1,0:T(8,128)} %get-tuple-element.82), channel_id=1, source_target_pairs={{0,3},{1,0},{2,1},{3,2},{4,7},{5,4},{6,5},{7,6},{8,11},{9,8},{10,9... | collective-permute-start | bytes 55304 | tf_op jit(solution)/shard_map/ppermute | solution.py:310
  116.5 15.4 %collective-permute-start.14 = (bf16[3,64,384]{2,1,0:T(8,128)(2,1)}, bf16[3,64,384]{2,1,0:T(8,128)(2,1)S(1)}, u32[]{:S(2)}, u32[]{:S(2)}) collective-permute-start(bf16[3,64,384]{2,1,0:T(8,128)(2,1)} %get-tuple-element.67), channel_id=1, source_target_pairs={{0,2},{1,3},{2,0},{3,1},{4,6},{5,7},{6,4},{7,5},{8,10},{9,11},{10,... | collective-permute-start | bytes 442376 | tf_op jit(solution)/shard_map/ppermute | solution.py:234
  118.3 21.8 %copy-start.7 = (bf16[3,64,384]{2,1,0:T(8,128)(2,1)}, bf16[3,64,384]{2,1,0:T(8,128)(2,1)S(1)}, u32[]{:S(2)}) copy-start(bf16[3,64,384]{2,1,0:T(8,128)(2,1)S(1)} %collective-permute-done.13.p1) | copy-start | bytes 442372
  118.3 21.8 %collective-permute-start.15 = (bf16[3,64,384]{2,1,0:T(8,128)(2,1)}, bf16[3,64,384]{2,1,0:T(8,128)(2,1)S(1)}, u32[]{:S(2)}, u32[]{:S(2)}) collective-permute-start(bf16[3,64,384]{2,1,0:T(8,128)(2,1)} %get-tuple-element.68), channel_id=1, source_target_pairs={{0,3},{1,0},{2,1},{3,2},{4,7},{5,4},{6,5},{7,6},{8,11},{9,8},{10,9... | collective-permute-start | bytes 442376 | tf_op jit(solution)/shard_map/ppermute | solution.py:234
  120.5 10.0 %copy-start.23 = (f32[72,64]{1,0:T(8,128)}, f32[72,64]{1,0:T(8,128)S(1)}, u32[]{:S(2)}) copy-start(f32[72,64]{1,0:T(8,128)S(1)} %collective-permute-done.23.r1) | copy-start | bytes 55300
  120.5 22.5 %collective-permute-start.8 = (bf16[3,64,384]{2,1,0:T(8,128)(2,1)S(1)}, bf16[3,64,384]{2,1,0:T(8,128)(2,1)S(1)}, u32[]{:S(2)}, u32[]{:S(2)}) collective-permute-start(bf16[3,64,384]{2,1,0:T(8,128)(2,1)S(1)} %copy-done.31), channel_id=1, source_target_pairs={{0,1},{1,2},{2,3},{3,0},{4,5},{5,6},{6,7},{7,4},{8,9},{9,10},{10,1... | collective-permute-start | bytes 442376 | tf_op jit(solution)/shard_map/ppermute | solution.py:234
  120.8 9.6 %copy-start.24 = (f32[72,64]{1,0:T(8,128)}, f32[72,64]{1,0:T(8,128)S(1)}, u32[]{:S(2)}) copy-start(f32[72,64]{1,0:T(8,128)S(1)} %collective-permute-done.24.r2) | copy-start | bytes 55300
  120.8 22.2 %collective-permute-start.9 = (bf16[3,64,384]{2,1,0:T(8,128)(2,1)S(1)}, bf16[3,64,384]{2,1,0:T(8,128)(2,1)S(1)}, u32[]{:S(2)}, u32[]{:S(2)}) collective-permute-start(bf16[3,64,384]{2,1,0:T(8,128)(2,1)S(1)} %copy-done.30), channel_id=1, source_target_pairs={{0,2},{1,3},{2,0},{3,1},{4,6},{5,7},{6,4},{7,5},{8,10},{9,11},{10,... | collective-permute-start | bytes 442376 | tf_op jit(solution)/shard_map/ppermute | solution.py:234
  127.1 3.3 %copy-start.25 = (f32[72,64]{1,0:T(8,128)}, f32[72,64]{1,0:T(8,128)S(1)}, u32[]{:S(2)}) copy-start(f32[72,64]{1,0:T(8,128)S(1)} %collective-permute-done.25.r3) | copy-start | bytes 55300
  127.1 16.1 %collective-permute-start.10 = (bf16[3,64,384]{2,1,0:T(8,128)(2,1)S(1)}, bf16[3,64,384]{2,1,0:T(8,128)(2,1)S(1)}, u32[]{:S(2)}, u32[]{:S(2)}) collective-permute-start(bf16[3,64,384]{2,1,0:T(8,128)(2,1)S(1)} %copy-done.29), channel_id=1, source_target_pairs={{0,3},{1,0},{2,1},{3,2},{4,7},{5,4},{6,5},{7,6},{8,11},{9,8},{10,9... | collective-permute-start | bytes 442376 | tf_op jit(solution)/shard_map/ppermute | solution.py:234
  131.9 8.2 %copy-start.11 = (bf16[3,64,384]{2,1,0:T(8,128)(2,1)}, bf16[3,64,384]{2,1,0:T(8,128)(2,1)S(1)}, u32[]{:S(2)}) copy-start(bf16[3,64,384]{2,1,0:T(8,128)(2,1)S(1)} %collective-permute-done.14.p2) | copy-start | bytes 442372
  131.9 14.3 %collective-permute-start.26 = (f32[72,64]{1,0:T(8,128)}, f32[72,64]{1,0:T(8,128)S(1)}, u32[]{:S(2)}, u32[]{:S(2)}) collective-permute-start(f32[72,64]{1,0:T(8,128)} %fold_z.1), channel_id=1, source_target_pairs={{0,128},{4,132},{8,136},{12,140},{16,144},{20,148},{24,152},{28,15... | collective-permute-start | bytes 55304 | tf_op jit(solution)/shard_map/ppermute | solution.py:312
  140.8 5.4 %copy-start.6 = (f32[72,64]{1,0:T(8,128)S(1)}, f32[72,64]{1,0:T(8,128)}, u32[]{:S(2)}) copy-start(f32[72,64]{1,0:T(8,128)} %fold_z.1) | copy-start | bytes 55300
  (11 other events, 7.4 us)

commit v2 on v1

v2 whole, which is shorter than its diff:
```python
import functools
import math

import jax
import jax.numpy as jnp
from jax import lax
from jax.experimental import pallas as pl
from jax.experimental.pallas import tpu as pltpu
from jax.sharding import PartitionSpec as P

BF = jnp.bfloat16
F32 = jnp.float32
ROWS = 3
OWN = 64
C = 256
J = 1440
K = 9
PART = 360
WIN = 384
PAD = 400
BLK = 32
SPAN = 48
REACH = 2
NSP = 5
X_OFF = 16
G_OFF = 8
LATE = 1
MIB = 1024 * 1024

VM = pl.BlockSpec(memory_space=pltpu.VMEM)
SM = pl.BlockSpec(memory_space=pltpu.SMEM)


def call(body, name, outs, n_in, scratch=(), limit=8, flops=0, nbytes=1_000_000):
    return pl.pallas_call(
        body,
        out_shape=[jax.ShapeDtypeStruct(s, d) for s, d in outs],
        in_specs=[SM] + [VM] * n_in,
        out_specs=[VM] * len(outs),
        scratch_shapes=list(scratch),
        compiler_params=pltpu.CompilerParams(vmem_limit_bytes=limit * MIB),
        cost_estimate=pl.CostEstimate(flops=flops, bytes_accessed=nbytes, transcendentals=0),
        name=name,
    )


def pack_body(idx, g, x, o0, o1, o2, o3, win):
    for r in range(2 * ROWS):
        v = g[r] if r < ROWS else x[r - ROWS]
        for h in range(4):
            a = PART * h - (G_OFF if r < ROWS else X_OFF)
            if a < 0:
                w = jnp.concatenate([v[:, J + a :], v[:, : WIN + a]], axis=1)
            elif a + WIN > J:
                w = jnp.concatenate([v[:, a:], v[:, : a + WIN - J]], axis=1)
            else:
                w = v[:, a : a + WIN]
            win[h, r] = w
    for s, o in enumerate((o0, o1, o2, o3)):
        o[...] = win[lax.bitwise_xor(idx[0], jnp.int32(s))]


def gather_parts(ch, refs, first, scr):
    for s, ref in enumerate(refs):
        src = lax.bitwise_xor(ch, jnp.int32(s))
        scr[:, pl.ds(pl.multiple_of(src * OWN, OWN), OWN), :] = ref[first : first + ROWS]


def asm_x_body(idx, p0, p1, p2, p3, out, near, far, scr):
    gather_parts(idx[0], (p0, p1, p2, p3), ROWS, scr)
    zeros = jnp.zeros((PAD - WIN, C), BF)
    for r in range(ROWS):
        out[r, :WIN, :] = scr[r].T
        out[r, WIN:, :] = zeros

    @pl.when(idx[1] == 0)
    def _():
        near[...] = out[1:]
        far[...] = out[:REACH]

    @pl.when(idx[1] != 0)
    def _():
        near[...] = out[:REACH]
        far[...] = out[1:]


def bands_body(idx, a, b, ta, tb):
    for n in range(ROWS * K):
        i, k = divmod(n, K)
        row = jnp.broadcast_to(a[n : n + 1, :], (BLK, 256))
        ta[i, k * BLK : (k + 1) * BLK, :] = pltpu.roll(row, 0, 1, stride=1, stride_axis=0).astype(BF)
    for n in range(ROWS * NSP):
        i, sp = divmod(n, NSP)
        row = jnp.broadcast_to(b[n : n + 1, :], (BLK, 512))
        tb[i, sp * BLK : (sp + 1) * BLK, :] = pltpu.roll(row, 0, 1, stride=1, stride_axis=0).astype(BF)


def forward_body(
    idx, x, near, far, ta, g0, g1, g2, g3, mix, yt, keep, send, basis, gt, ws
):
    ch = idx[0]
    first = idx[1] == 0

    def row(m, at):
        if REACH <= m < REACH + ROWS:
            return x[m - REACH, pl.ds(at, SPAN), :]
        n = m if m < REACH else m - REACH - ROWS
        a = near[n, pl.ds(at, SPAN), :]
        b = far[n, pl.ds(at, SPAN), :]
        return jnp.where(first, b, a) if m < REACH else jnp.where(first, a, b)

    zeros = jnp.zeros((256 - NSP * SPAN, C), BF)

    @pl.loop(0, WIN // BLK)
    def _(b):
        at = pl.multiple_of(b * BLK, BLK)
        rows = [row(m, at) for m in range(ROWS + 2 * REACH)]
        for i in range(ROWS):
            rhs = jnp.concatenate(rows[i : i + NSP] + [zeros], axis=0)
            out = jnp.dot(ta[i], rhs, preferred_element_type=F32).astype(BF)
            for k in range(K):
                basis[pl.ds(pl.multiple_of(i * WIN + at, BLK), BLK), k * C : (k + 1) * C] = out[k * BLK : (k + 1) * BLK]

    m = mix[...]
    for i in range(ROWS):
        y = jnp.dot(basis[i * WIN : (i + 1) * WIN, :], m, preferred_element_type=F32)
        yt[i] = y.T.astype(BF)

    gather_parts(ch, (g0, g1, g2, g3), 0, gt)
    lane = lax.broadcasted_iota(jnp.int32, (C, WIN), 1)
    own = (lane >= G_OFF) & (lane < G_OFF + PART)
    g = jnp.concatenate([jnp.where(own, gt[r].astype(F32), 0.0).astype(BF) for r in range(ROWS)], axis=1)
    low = lax.broadcasted_iota(jnp.int32, (32, 8, C), 1) < 4

    def weight(k):
        return jnp.dot(g, basis[:, k * C : (k + 1) * C], preferred_element_type=F32).T.reshape(32, 8, C)

    for m in range(5):
        wa = weight(2 * m)
        wb = weight(2 * m + 1) if 2 * m + 1 < K else wa
        even = jnp.where(low, wa, pltpu.roll(wb, 4, 1))
        odd = jnp.where(low, pltpu.roll(wa, 4, 1), wb)
        keep[:, 8 * m : 8 * m + 8, :] = jnp.where(first, even, odd)
        ws[:, 8 * m : 8 * m + 8, :] = jnp.where(first, odd, even)
    send[...] = ws[...].reshape(32 * 40, C).astype(BF)


def backward_body(idx, g0, g1, g2, g3, tb, mix, mid, near, far, gt, bg, rim):
    gather_parts(idx[0], (g0, g1, g2, g3), 0, gt)
    bg[:, WIN:, :] = jnp.zeros((ROWS, PAD - WIN, K * C), BF)
    for i in range(ROWS):
        g = gt[i].T
        for k in range(K):
            bg[i, :WIN, k * C : (k + 1) * C] = lax.dot_general(
                g, mix[k * C : (k + 1) * C, :], (((1,), (1,)), ((), ())), preferred_element_type=F32
            ).astype(BF)
    zeros = jnp.zeros((512 - K * SPAN, C), BF)

    @pl.loop(0, WIN // BLK)
    def _(b):
        at = pl.multiple_of(b * BLK, BLK)
        acc = [None] * (ROWS + 2 * REACH)
        for i in range(ROWS):
            rhs = jnp.concatenate(
                [bg[i, pl.ds(at, SPAN), k * C : (k + 1) * C] for k in range(K)] + [zeros], axis=0
            )
            out = jnp.dot(tb[i], rhs, preferred_element_type=F32)
            for sp in range(NSP):
                part = out[sp * BLK : (sp + 1) * BLK]
                acc[i + sp] = part if acc[i + sp] is None else acc[i + sp] + part
        for n in range(2):
            rim[0, n, pl.ds(at, BLK), :] = acc[n].astype(BF)
            rim[1, n, pl.ds(at, BLK), :] = acc[ROWS + REACH + n].astype(BF)
        for n in range(ROWS):
            mid[n, pl.ds(at, BLK), :] = acc[REACH + n]

    near[...] = rim[1 - idx[1]]
    far[...] = rim[idx[1]]


def join_body(idx, mid, near, far, yt, o0, o1, o2, o3, rest, scr):
    first = idx[1] == 0
    for r in range(ROWS):
        v = mid[r]
        if r < REACH:
            v = v + jnp.where(first, far[r], near[r]).astype(F32)
        if r >= ROWS - REACH:
            n = r - (ROWS - REACH)
            v = v + jnp.where(first, near[n], far[n]).astype(F32)
        if r < ROWS - LATE:
            scr[r] = v.T.astype(BF)
        else:
            rest[r - (ROWS - LATE)] = v.T.astype(BF)
    for s, o in enumerate((o0, o1, o2, o3)):
        to = lax.bitwise_xor(idx[0], jnp.int32(s))
        at = pl.ds(pl.multiple_of(to * OWN, OWN), OWN)
        o[:ROWS] = yt[:, at, :]
        o[ROWS:] = scr[:, at, :]


def fold_lat_body(idx, got, rest, o0, o1, o2, o3, ws):
    total = jnp.sum(got[...].astype(F32).reshape(32, 40, C), axis=0)
    for h in range(4):
        cols = total[:, h * OWN : (h + 1) * OWN]
        v = jnp.concatenate([cols[8 * m : 8 * m + 8] for m in range(5)] + [jnp.zeros((8, OWN), F32)], axis=1)
        high = v.astype(BF).astype(F32)
        ws[h] = jnp.concatenate([high, v - high], axis=0).astype(BF)
    for s, o in enumerate((o0, o1, o2, o3)):
        to = lax.bitwise_xor(idx[0], jnp.int32(s))
        for r in range(LATE):
            o[r * OWN : (r + 1) * OWN, :] = rest[r, pl.ds(pl.multiple_of(to * OWN, OWN), OWN), :]
        o[LATE * OWN :, :] = ws[to]


def unpack_body(scale, idx, a0, a1, a2, a3, b0, b1, b2, b3, y, g, w, sa, sb):
    for s, (a, b) in enumerate(((a0, b0), (a1, b1), (a2, b2), (a3, b3))):
        src = lax.bitwise_xor(idx[0], jnp.int32(s))
        sa[src] = a[...]
        sb[src] = b[...]
    for r in range(ROWS):
        y[r] = jnp.concatenate([sa[h, r][:, G_OFF : G_OFF + PART] for h in range(4)], axis=1)
    for r in range(ROWS - LATE):
        g[r] = jnp.concatenate([sa[h, ROWS + r][:, :PART] for h in range(4)], axis=1)
    for r in range(LATE):
        g[ROWS - LATE + r] = jnp.concatenate([sb[h, r * OWN : (r + 1) * OWN, :PART] for h in range(4)], axis=1)
    total = jnp.zeros((8, WIN), F32)
    for h in range(4):
        v = sb[h, LATE * OWN :, :].astype(F32)
        total = total + (v[:8] + v[8:])
    total = total * scale
    for k in range(K):
        m, odd = divmod(k, 2)
        for r in range(4):
            row = 4 * odd + r
            w[r, k : k + 1, :] = total[row : row + 1, m * OWN : (m + 1) * OWN]


def fold_core_body(idx, keep, got, out):
    out[...] = (keep[...] + got[...].astype(F32)).astype(BF)


def swap_ch(mask):
    return [(i, i ^ mask) for i in range(4)]


def swap_lat():
    near = [(i, i ^ 1) for i in range(64)]
    far = []
    for i in range(1, 63, 2):
        far += [(i, i + 1), (i + 1, i)]
    return near, far


def local(x_field, cotangent, halo_rows, filters, mixing):
    lat = lax.axis_index("lat")
    ch = lax.axis_index("ch")
    idx = jnp.stack([ch, lat % 2]).astype(jnp.int32)
    mix2 = mixing.reshape(K * C, C)
    pair = ((2 * ROWS, OWN, WIN), BF)

    def exchange(parts):
        got = {s: lax.ppermute(parts[s], "ch", swap_ch(s)) for s in (2, 1, 3)}
        return [parts[0], got[1], got[2], got[3]]

    parts = exchange(
        call(pack_body, "pack", [pair] * 4, 2, [pltpu.VMEM((4, 2 * ROWS, OWN, WIN), BF)])(idx, cotangent, x_field)
    )

    want = lat * ROWS + jnp.arange(ROWS, dtype=jnp.int32)[:, None] - REACH + jnp.arange(NSP, dtype=jnp.int32)[None, :]
    hit = (halo_rows[:, :, None] == want[:, None, :]) & (halo_rows[:, :, None] >= 0)
    taps = jnp.sum(jnp.where(hit[:, :, None, :, None], filters.astype(F32)[:, :, :, None, :], 0.0), axis=1)
    ntap = taps.shape[-1]
    a = jnp.pad(taps, ((0, 0),) * 3 + ((0, SPAN - ntap),)).reshape(ROWS * K, NSP * SPAN)
    a = jnp.pad(a, ((0, 0), (0, 256 - NSP * SPAN)))
    b = jnp.pad(taps[..., ::-1], ((0, 0),) * 3 + ((1, SPAN - ntap - 1),))
    b = jnp.transpose(b, (0, 2, 1, 3)).reshape(ROWS * NSP, K * SPAN)
    b = jnp.pad(b, ((0, 0), (0, 512 - K * SPAN)))
    ta, tb = call(
        bands_body, "bands", [((ROWS, K * BLK, 256), BF), ((ROWS, NSP * BLK, 512), BF)], 2
    )(idx, a, b)

    parts, ta, tb = lax.optimization_barrier((parts, ta, tb))
    lon = (ROWS, PAD, C)
    rim = (REACH, PAD, C)
    x_lon, x_near, x_far = call(
        asm_x_body, "asm_x", [(lon, BF), (rim, BF), (rim, BF)], 4, [pltpu.VMEM((ROWS, C, WIN), BF)]
    )(idx, *parts)
    to_near, to_far = swap_lat()
    x_far = lax.ppermute(x_far, "lat", to_far)
    x_near = lax.ppermute(x_near, "lat", to_near)

    tb, _ = lax.optimization_barrier((tb, x_lon))
    mid, near, far = call(
        backward_body,
        "backward",
        [((ROWS, WIN, C), F32), ((REACH, WIN, C), BF), ((REACH, WIN, C), BF)],
        6,
        [
            pltpu.VMEM((ROWS, C, WIN), BF),
            pltpu.VMEM((ROWS, PAD, K * C), BF),
            pltpu.VMEM((2, REACH, WIN, C), BF),
        ],
        limit=20,
        flops=8_000_000_000,
        nbytes=5_000_000,
    )(idx, *parts, tb, mix2)
    far = lax.ppermute(far, "lat", to_far)
    near = lax.ppermute(near, "lat", to_near)

    ta, mid = lax.optimization_barrier((ta, mid))
    yt, keep, send = call(
        forward_body,
        "forward",
        [((ROWS, C, WIN), BF), ((32, 40, C), F32), ((32 * 40, C), BF)],
        9,
        [pltpu.VMEM((ROWS * WIN, K * C), BF), pltpu.VMEM((ROWS, C, WIN), BF), pltpu.VMEM((32, 40, C), F32)],
        limit=28,
        flops=8_000_000_000,
        nbytes=9_000_000,
    )(idx, x_lon, x_near, x_far, ta, *parts, mix2)
    yt, send, near, far = lax.optimization_barrier((yt, send, near, far))
    got = lax.ppermute(send, "lat", to_near)
    early = ((2 * ROWS - LATE, OWN, WIN), BF)
    late = (LATE * OWN + 16, WIN)
    *outs, rest = call(
        join_body, "join", [early] * 4 + [((LATE, C, WIN), BF)], 4, [pltpu.VMEM((ROWS - LATE, C, WIN), BF)], limit=10
    )(idx, mid, near, far, yt)
    got, _ = lax.optimization_barrier((got, outs[0]))
    outs = exchange(outs)
    (half,) = call(fold_core_body, "fold_core", [((32 * 40, C), BF)], 2)(idx, keep.reshape(32 * 40, C), got)
    groups = [[2 * q + core for q in range(32)] for core in range(2)]
    got = lax.all_to_all(half, "lat", 0, 0, axis_index_groups=groups, tiled=True)
    last = exchange(call(fold_lat_body, "fold_lat", [(late, BF)] * 4, 2, [pltpu.VMEM((4, 16, WIN), BF)])(idx, got, rest))
    return call(
        functools.partial(unpack_body, 1.0 / math.sqrt(64 * ROWS * J)),
        "unpack",
        [((ROWS, OWN, J), BF), ((ROWS, OWN, J), BF), ((4, K, OWN), F32)],
        8,
        [pltpu.VMEM((4, 2 * ROWS - LATE, OWN, WIN), BF), pltpu.VMEM((4,) + late, BF)],
    )(idx, *outs, *last)


def solution(mesh):
    return jax.shard_map(
        local,
        mesh=mesh,
        in_specs=(
            P("lat", "ch", None),
            P("lat", "ch", None),
            P("lat", None),
            P("lat", None, None, None),
            P(),
        ),
        out_specs=(P("lat", "ch", None), P("lat", "ch", None), P("lat", None, "ch")),
        check_vma=False,
    )
```

time: 147 us -> 114 us (0.78)
  Pallas kernels: 44.5 us -> 20.9 us
  starting transfers between devices: 60.2 us -> 48.5 us
  waiting for transfers between devices: 31 us -> 40.2 us
  local copies, waits for them, and re-layouts: 9.32 us -> 3.45 us
    ppermute x27 -> x14, starting transfers between devices: 60.2 us -> 38.8 us  [the longest x9 25.6 us: exchange(): got = {s: lax.ppermute(parts[s], 'ch', swap_ch(s)) for s in (2, 1, 3)}]
    pallas_call x11 -> x6, Pallas kernels: 32.1 us -> 13.4 us  [the longest x1 7.23 us: local(): call(forward_body, 'forward', [((ROWS, C, WIN), BF), ((32, 40, C), F32),...]
    all_to_all x0 -> x1, waiting for transfers between devices: none -> 10.9 us  [local(): lax.all_to_all(half, 'lat', 0, 0, axis_index_groups=groups, tiled=True)]
    all_to_all x0 -> x1, starting transfers between devices: none -> 9.68 us  [local(): lax.all_to_all(half, 'lat', 0, 0, axis_index_groups=groups, tiled=True)]
    unnamed x66 -> x12, local copies, waits for them, and re-layouts: 6.89 us -> 2.25 us
    pallas_call x1, Pallas kernels: 7.93 us -> 5.76 us  [local(): call(backward_body, 'backward', [((ROWS, WIN, C), F32), ((REACH, WIN, C),...]
    ppermute x27 -> x14, waiting for transfers between devices: 31 us -> 29.3 us  [the longest x9 28 us: exchange(): got = {s: lax.ppermute(parts[s], 'ch', swap_ch(s)) for s in (2, 1, 3)}]
    pallas_call x1, Pallas kernels: 2.5 us -> 0.85 us  [local(): call(asm_x_body, 'asm_x', [(lon, BF), (rim, BF), (rim, BF)], 4, [pltpu.VM...]
  transfers between devices with their start and end apart: 27 -> 15, of which waited for: 10 -> 7; matrix products, arithmetic and copies ran while one was open for 1% -> 1% of each run, Pallas kernels for 22% -> 13%
where the time goes in v2:
time: 114 us
  starting transfers between devices  48.5 us (43%)
  waiting for transfers between devices  40.2 us (35%)
  Pallas kernels  20.9 us (18%)
  local copies, waits for them, and re-layouts  3.45 us (3%)
    ppermute x9, waiting for transfers between devices, exchange(): got = {s: lax.ppermute(parts[s], 'ch', swap_ch(s)) for s in (2, 1, 3)}  28 us
    ppermute x9, starting transfers between devices, exchange(): got = {s: lax.ppermute(parts[s], 'ch', swap_ch(s)) for s in (2, 1, 3)}  25.6 us
    all_to_all x1, waiting for transfers between devices, local(): lax.all_to_all(half, 'lat', 0, 0, axis_index_groups=groups, tiled=True)  10.9 us
    all_to_all x1, starting transfers between devices, local(): lax.all_to_all(half, 'lat', 0, 0, axis_index_groups=groups, tiled=True)  9.68 us
    pallas_call x1, Pallas kernels, local(): call(forward_body, 'forward', [((ROWS, C, WIN), BF), ((32, 40, C), F32),...  7.23 us
    ppermute x1, starting transfers between devices, local(): x_near = lax.ppermute(x_near, 'lat', to_near)  6.34 us
    pallas_call x1, Pallas kernels, local(): call(backward_body, 'backward', [((ROWS, WIN, C), F32), ((REACH, WIN, C),...  5.76 us
    ppermute x1, starting transfers between devices, local(): far = lax.ppermute(far, 'lat', to_far)  3.58 us
  transfers between devices with their start and end apart: 15, of which 7 were waited for; matrix products, arithmetic and copies ran while one was open for 1% of the time, Pallas kernels for 13%

profile of v2, /device:TPU:1, one launch (start us, length us, event | category | flops | bytes accessed | tf_op | source)
XLA Modules:
  0.0 114.2 jit_solution(17423507395262536111)
XLA Ops:
  0.7 0.1 pad_add_fusion.idx
  0.7 1.1 copy-done
  1.8 1.1 copy-done.1
  2.9 1.2 %pack.1 = (bf16[6,64,384]{2,1,0:T(8,128)(2,1)S(1)}, bf16[6,64,384]{2,1,0:T(8,128)(2,1)S(1)}, bf16[6,64,384]{2,1,0:T(8,128)(2,1)S(1)}, bf16[6,64,384]{2,1,0:T(8,128)(2,1)S(1)}) custom-call(s32[2]{0:T(128)S(1)} %pad_add_fusion.idx, bf16[3,64,1440]{2,1,0:T(8,128)(2,1)S(1)} %copy-done, bf16[3,64,1440]{2,1,0:T(8,128)(2,1)S(1)} %copy-done.1), custom_call_target="tpu_custom_call" | custom-call | bytes 1000000 | tf_op jit(solution)/shard_map/pack/pallas_call | solution.py:266
  4.1 3.9 %collective-permute-start = (bf16[6,64,384]{2,1,0:T(8,128)(2,1)S(1)}, bf16[6,64,384]{2,1,0:T(8,128)(2,1)S(1)}, u32[]{:S(2)}, u32[]{:S(2)}) collective-permute-start(bf16[6,64,384]{2,1,0:T(8,128)(2,1)S(1)} %get-tuple-element.42), channel_id=1, source_target_pairs={{0,1},{1,0},{2,3},{3,2},{4,5},{5,4},{6,7},{7,6},{8,9},{9,8},{10,11... | collective-permute-start | bytes 884744 | tf_op jit(solution)/shard_map/ppermute | solution.py:262
  8.0 5.1 %collective-permute-start.1 = (bf16[6,64,384]{2,1,0:T(8,128)(2,1)S(1)}, bf16[6,64,384]{2,1,0:T(8,128)(2,1)S(1)}, u32[]{:S(2)}, u32[]{:S(2)}) collective-permute-start(bf16[6,64,384]{2,1,0:T(8,128)(2,1)S(1)} %get-tuple-element.43), channel_id=1, source_target_pairs={{0,2},{1,3},{2,0},{3,1},{4,6},{5,7},{6,4},{7,5},{8,10},{9,11},{10,... | collective-permute-start | bytes 884744 | tf_op jit(solution)/shard_map/ppermute | solution.py:262
  13.1 0.0 collective-permute-start.2
  13.1 0.1 copy.14
  13.2 0.1 copy.15
  13.3 0.2 select_reduce_fusion
  13.5 0.2 rev.3
  13.7 0.0 copy-start.2
  13.8 0.1 reshape.50
  13.9 0.1 pad_bitcast_fusion
  14.0 0.1 reshape.51
  14.1 0.8 bands.1
  15.0 18.0 %collective-permute-done.p1.g1 = bf16[6,64,384]{2,1,0:T(8,128)(2,1)S(1)} collective-permute-done((bf16[6,64,384]{2,1,0:T(8,128)(2,1)S(1)}, bf16[6,64,384]{2,1,0:T(8,128)(2,1)S(1)}, u32[]{:S(2)}, u32[]{:S(2)}) %collective-permute-start) | collective-permute-done | bytes 294944 | tf_op jit(solution)/shard_map/ppermute | solution.py:262
  33.0 0.1 collective-permute-done.1.p2.g2
  33.2 0.6 collective-permute-done.2.p3.g3
  33.8 0.9 asm_x.1
  34.6 6.3 %collective-permute-start.3 = (bf16[2,400,256]{2,1,0:T(8,128)(2,1)S(1)}, bf16[2,400,256]{2,1,0:T(8,128)(2,1)S(1)}, u32[]{:S(2)}, u32[]{:S(2)}) collective-permute-start(bf16[2,400,256]{2,1,0:T(8,128)(2,1)S(1)} %get-tuple-element.57), channel_id=1, source_target_pairs={{0,4},{4,0},{8,12},{12,8},{16,20},{20,16},{24,28},{28,24},{32,36},... | collective-permute-start | bytes 1228808 | tf_op jit(solution)/shard_map/ppermute | solution.py:290
  41.0 3.1 %collective-permute-start.4 = (bf16[2,400,256]{2,1,0:T(8,128)(2,1)S(1)}, bf16[2,400,256]{2,1,0:T(8,128)(2,1)S(1)}, u32[]{:S(2)}, u32[]{:S(2)}) collective-permute-start(bf16[2,400,256]{2,1,0:T(8,128)(2,1)S(1)} %get-tuple-element.58), channel_id=1, source_target_pairs={{4,8},{8,4},{12,16},{16,12},{20,24},{24,20},{28,32},{32,28},{36,40... | collective-permute-start | bytes 1228808 | tf_op jit(solution)/shard_map/ppermute | solution.py:289
  44.1 5.8 %backward.1 = (f32[3,384,256]{2,1,0:T(8,128)S(1)}, bf16[2,384,256]{2,1,0:T(8,128)(2,1)S(1)}, bf16[2,384,256]{2,1,0:T(8,128)(2,1)S(1)}) custom-call(s32[2]{0:T(128)S(1)} %pad_add_fusion.idx, bf16[6,64,384]{2,1,0:T(8,128)(2,1)S(1)} %get-tuple-element.48.p0.g0, bf16[6,64,384]{2,1,0:T(8,128)(2,1)S(1)} %collective-permute-done.p1.g1, ...), custom_call_target="tpu_custom_call" | custom-call | flops 8000000000 | bytes 5000000 | tf_op jit(solution)/shard_map/backward/pallas_call | solution.py:293
  49.9 0.1 collective-permute-start.5
  50.0 3.6 %collective-permute-start.6 = (bf16[2,384,256]{2,1,0:T(8,128)(2,1)S(1)}, bf16[2,384,256]{2,1,0:T(8,128)(2,1)S(1)}, u32[]{:S(2)}, u32[]{:S(2)}) collective-permute-start(bf16[2,384,256]{2,1,0:T(8,128)(2,1)S(1)} %get-tuple-element.63), channel_id=1, source_target_pairs={{4,8},{8,4},{12,16},{16,12},{20,24},{24,20},{28,32},{32,28},{36,40... | collective-permute-start | bytes 1179656 | tf_op jit(solution)/shard_map/ppermute | solution.py:307
  53.6 0.0 collective-permute-done.3.near
  53.6 0.0 collective-permute-done.4.far
  53.6 7.2 %forward.1 = (bf16[3,256,384]{2,1,0:T(8,128)(2,1)S(1)}, f32[32,40,256]{2,1,0:T(8,128)S(1)}, bf16[1280,256]{1,0:T(8,128)(2,1)S(1)}) custom-call(s32[2]{0:T(128)S(1)} %pad_add_fusion.idx, bf16[3,400,256]{2,1,0:T(8,128)(2,1)S(1)} %get-tuple-element.53.x, bf16[2,400,256]{2,1,0:T(8,128)(2,1)S(1)} %collective-permute-done.3.near, ...), custom_call_target="tpu_custom_call" | custom-call | flops 8000000000 | bytes 9000000 | tf_op jit(solution)/shard_map/forward/pallas_call | solution.py:311
  60.8 0.0 collective-permute-done.5.near
  60.8 0.1 collective-permute-start.10
  60.9 0.8 join.1
  61.8 1.2 %collective-permute-done.10.got = bf16[1280,256]{1,0:T(8,128)(2,1)S(1)} collective-permute-done((bf16[1280,256]{1,0:T(8,128)(2,1)S(1)}, bf16[1280,256]{1,0:T(8,128)(2,1)S(1)}, u32[]{:S(2)}, u32[]{:S(2)}) %collective-permute-start.10) | collective-permute-done | bytes 655392 | tf_op jit(solution)/shard_map/ppermute | solution.py:322
  63.0 1.5 %fold_core.1 = bf16[1280,256]{1,0:T(8,128)(2,1)} custom-call(s32[2]{0:T(128)S(1)} %pad_add_fusion.idx, f32[1280,256]{1,0:T(8,128)S(1)} %bitcast.9, bf16[1280,256]{1,0:T(8,128)(2,1)S(1)} %collective-permute-done.10.got), custom_call_target="tpu_custom_call" | custom-call | bytes 1000000 | tf_op jit(solution)/shard_map/fold_core/pallas_call | solution.py:330
  64.6 9.7 %all-to-all-start = ((bf16[32,40,256]{2,1,0:T(8,128)(2,1)}), bf16[32,40,256]{2,1,0:T(8,128)(2,1)S(1)}, u32[]{:S(2)}, u32[]{:S(2)}) async-start(bf16[32,40,256]{2,1,0:T(8,128)(2,1)} %bitcast.5), calls=%async_computation | async-start | bytes 1310720 | tf_op jit(solution)/shard_map/all_to_all | solution.py:332
  74.2 2.0 %collective-permute-start.7 = (bf16[5,64,384]{2,1,0:T(8,128)(2,1)S(1)}, bf16[5,64,384]{2,1,0:T(8,128)(2,1)S(1)}, u32[]{:S(2)}, u32[]{:S(2)}) collective-permute-start(bf16[5,64,384]{2,1,0:T(8,128)(2,1)S(1)} %get-tuple-element.68), channel_id=1, source_target_pairs={{0,1},{1,0},{2,3},{3,2},{4,5},{5,4},{6,7},{7,6},{8,9},{9,8},{10,11... | collective-permute-start | bytes 737288 | tf_op jit(solution)/shard_map/ppermute | solution.py:262
  76.2 3.8 %collective-permute-start.8 = (bf16[5,64,384]{2,1,0:T(8,128)(2,1)S(1)}, bf16[5,64,384]{2,1,0:T(8,128)(2,1)S(1)}, u32[]{:S(2)}, u32[]{:S(2)}) collective-permute-start(bf16[5,64,384]{2,1,0:T(8,128)(2,1)S(1)} %get-tuple-element.69), channel_id=1, source_target_pairs={{0,2},{1,3},{2,0},{3,1},{4,6},{5,7},{6,4},{7,5},{8,10},{9,11},{10,... | collective-permute-start | bytes 737288 | tf_op jit(solution)/shard_map/ppermute | solution.py:262
  80.0 0.0 collective-permute-start.9
  80.0 10.9 %all-to-all-done = bf16[32,40,256]{2,1,0:T(8,128)(2,1)S(1)} async-done(((bf16[32,40,256]{2,1,0:T(8,128)(2,1)}), bf16[32,40,256]{2,1,0:T(8,128)(2,1)S(1)}, u32[]{:S(2)}, u32[]{:S(2)}) %all-to-all-start) | async-done | bytes 655392 | tf_op jit(solution)/shard_map/all_to_all | solution.py:332
  90.9 0.7 fold_lat.1
  91.6 0.1 collective-permute-start.11
  91.7 5.6 %collective-permute-start.12 = (bf16[80,384]{1,0:T(8,128)(2,1)S(1)}, bf16[80,384]{1,0:T(8,128)(2,1)S(1)}, u32[]{:S(2)}, u32[]{:S(2)}) collective-permute-start(bf16[80,384]{1,0:T(8,128)(2,1)S(1)} %get-tuple-element.77), channel_id=1, source_target_pairs={{0,2},{1,3},{2,0},{3,1},{4,6},{5,7},{6,4},{7,5},{8,10},{9,11},{10,... | collective-permute-start | bytes 184328 | tf_op jit(solution)/shard_map/ppermute | solution.py:262
  97.3 0.0 collective-permute-done.7.a1
  97.3 5.1 %collective-permute-start.13 = (bf16[80,384]{1,0:T(8,128)(2,1)S(1)}, bf16[80,384]{1,0:T(8,128)(2,1)S(1)}, u32[]{:S(2)}, u32[]{:S(2)}) collective-permute-start(bf16[80,384]{1,0:T(8,128)(2,1)S(1)} %get-tuple-element.78), channel_id=1, source_target_pairs={{0,3},{1,2},{2,1},{3,0},{4,7},{5,6},{6,5},{7,4},{8,11},{9,10},{10,... | collective-permute-start | bytes 184328 | tf_op jit(solution)/shard_map/ppermute | solution.py:262
  102.5 5.7 %collective-permute-done.8.a2 = bf16[5,64,384]{2,1,0:T(8,128)(2,1)S(1)} collective-permute-done((bf16[5,64,384]{2,1,0:T(8,128)(2,1)S(1)}, bf16[5,64,384]{2,1,0:T(8,128)(2,1)S(1)}, u32[]{:S(2)}, u32[]{:S(2)}) %collective-permute-start.8) | collective-permute-done | bytes 245792 | tf_op jit(solution)/shard_map/ppermute | solution.py:262
  108.1 0.0 collective-permute-done.9.a3
  108.1 3.6 %collective-permute-done.11.b1 = bf16[80,384]{1,0:T(8,128)(2,1)S(1)} collective-permute-done((bf16[80,384]{1,0:T(8,128)(2,1)S(1)}, bf16[80,384]{1,0:T(8,128)(2,1)S(1)}, u32[]{:S(2)}, u32[]{:S(2)}) %collective-permute-start.11) | collective-permute-done | bytes 61472 | tf_op jit(solution)/shard_map/ppermute | solution.py:262
  111.7 1.9 %unpack.1 = (bf16[3,64,1440]{2,1,0:T(8,128)(2,1)}, bf16[3,64,1440]{2,1,0:T(8,128)(2,1)}, f32[4,9,64]{2,1,0:T(8,128)S(1)}) custom-call(s32[2]{0:T(128)S(1)} %pad_add_fusion.idx, bf16[5,64,384]{2,1,0:T(8,128)(2,1)S(1)} %get-tuple-element.67.a0, bf16[5,64,384]{2,1,0:T(8,128)(2,1)S(1)} %collective-permute-done.7.a1, ...), custom_call_target="tpu_custom_call" | custom-call | bytes 1000000 | tf_op jit(solution)/shard_map/unpack/pallas_call | solution.py:334
  113.6 0.6 copy.18
  (20 shorter events, 0.1 us)
Async XLA Ops:
  0.6 12.4 %copy-start.4 = (s32[3,5]{1,0:T(4,128)S(1)}, s32[3,5]{1,0:T(4,128)}, u32[]{:S(2)}) copy-start(s32[3,5]{1,0:T(4,128)} %param.7) | copy-start | bytes 184
  0.7 1.1 copy-start
  1.8 1.1 copy-start.1
  2.9 10.5 %copy-start.3 = (bf16[3,5,9,16]{3,0,2,1:T(4,128)(2,1)S(1)}, bf16[3,5,9,16]{3,0,2,1:T(4,128)(2,1)}, u32[]{:S(2)}) copy-start(bf16[3,5,9,16]{3,0,2,1:T(4,128)(2,1)} %param.8) | copy-start | bytes 12964
  4.1 29.0 %collective-permute-start = (bf16[6,64,384]{2,1,0:T(8,128)(2,1)S(1)}, bf16[6,64,384]{2,1,0:T(8,128)(2,1)S(1)}, u32[]{:S(2)}, u32[]{:S(2)}) collective-permute-start(bf16[6,64,384]{2,1,0:T(8,128)(2,1)S(1)} %get-tuple-element.42), channel_id=1, source_target_pairs={{0,1},{1,0},{2,3},{3,2},{4,5},{5,4},{6,7},{7,6},{8,9},{9,8},{10,11... | collective-permute-start | bytes 884744 | tf_op jit(solution)/shard_map/ppermute | solution.py:262
  8.0 25.2 %collective-permute-start.1 = (bf16[6,64,384]{2,1,0:T(8,128)(2,1)S(1)}, bf16[6,64,384]{2,1,0:T(8,128)(2,1)S(1)}, u32[]{:S(2)}, u32[]{:S(2)}) collective-permute-start(bf16[6,64,384]{2,1,0:T(8,128)(2,1)S(1)} %get-tuple-element.43), channel_id=1, source_target_pairs={{0,2},{1,3},{2,0},{3,1},{4,6},{5,7},{6,4},{7,5},{8,10},{9,11},{10,... | collective-permute-start | bytes 884744 | tf_op jit(solution)/shard_map/ppermute | solution.py:262
  13.1 20.7 %collective-permute-start.2 = (bf16[6,64,384]{2,1,0:T(8,128)(2,1)S(1)}, bf16[6,64,384]{2,1,0:T(8,128)(2,1)S(1)}, u32[]{:S(2)}, u32[]{:S(2)}) collective-permute-start(bf16[6,64,384]{2,1,0:T(8,128)(2,1)S(1)} %get-tuple-element.44), channel_id=1, source_target_pairs={{0,3},{1,2},{2,1},{3,0},{4,7},{5,6},{6,5},{7,4},{8,11},{9,10},{10,... | collective-permute-start | bytes 884744 | tf_op jit(solution)/shard_map/ppermute | solution.py:262
  13.7 30.4 %copy-start.2 = (bf16[9,256,256]{2,1,0:T(8,128)(2,1)S(1)}, bf16[9,256,256]{2,1,0:T(8,128)(2,1)}, u32[]{:S(2)}) copy-start(bf16[9,256,256]{2,1,0:T(8,128)(2,1)} %param.9) | copy-start | bytes 3538948
  34.6 18.9 %collective-permute-start.3 = (bf16[2,400,256]{2,1,0:T(8,128)(2,1)S(1)}, bf16[2,400,256]{2,1,0:T(8,128)(2,1)S(1)}, u32[]{:S(2)}, u32[]{:S(2)}) collective-permute-start(bf16[2,400,256]{2,1,0:T(8,128)(2,1)S(1)} %get-tuple-element.57), channel_id=1, source_target_pairs={{0,4},{4,0},{8,12},{12,8},{16,20},{20,16},{24,28},{28,24},{32,36},... | collective-permute-start | bytes 1228808 | tf_op jit(solution)/shard_map/ppermute | solution.py:290
  41.0 12.6 %collective-permute-start.4 = (bf16[2,400,256]{2,1,0:T(8,128)(2,1)S(1)}, bf16[2,400,256]{2,1,0:T(8,128)(2,1)S(1)}, u32[]{:S(2)}, u32[]{:S(2)}) collective-permute-start(bf16[2,400,256]{2,1,0:T(8,128)(2,1)S(1)} %get-tuple-element.58), channel_id=1, source_target_pairs={{4,8},{8,4},{12,16},{16,12},{20,24},{24,20},{28,32},{32,28},{36,40... | collective-permute-start | bytes 1228808 | tf_op jit(solution)/shard_map/ppermute | solution.py:289
  49.9 10.9 %collective-permute-start.5 = (bf16[2,384,256]{2,1,0:T(8,128)(2,1)S(1)}, bf16[2,384,256]{2,1,0:T(8,128)(2,1)S(1)}, u32[]{:S(2)}, u32[]{:S(2)}) collective-permute-start(bf16[2,384,256]{2,1,0:T(8,128)(2,1)S(1)} %get-tuple-element.62), channel_id=1, source_target_pairs={{0,4},{4,0},{8,12},{12,8},{16,20},{20,16},{24,28},{28,24},{32,36},... | collective-permute-start | bytes 1179656 | tf_op jit(solution)/shard_map/ppermute | solution.py:308
  50.0 10.9 %collective-permute-start.6 = (bf16[2,384,256]{2,1,0:T(8,128)(2,1)S(1)}, bf16[2,384,256]{2,1,0:T(8,128)(2,1)S(1)}, u32[]{:S(2)}, u32[]{:S(2)}) collective-permute-start(bf16[2,384,256]{2,1,0:T(8,128)(2,1)S(1)} %get-tuple-element.63), channel_id=1, source_target_pairs={{4,8},{8,4},{12,16},{16,12},{20,24},{24,20},{28,32},{32,28},{36,40... | collective-permute-start | bytes 1179656 | tf_op jit(solution)/shard_map/ppermute | solution.py:307
  60.8 2.2 %collective-permute-start.10 = (bf16[1280,256]{1,0:T(8,128)(2,1)S(1)}, bf16[1280,256]{1,0:T(8,128)(2,1)S(1)}, u32[]{:S(2)}, u32[]{:S(2)}) collective-permute-start(bf16[1280,256]{1,0:T(8,128)(2,1)S(1)} %get-tuple-element.72), channel_id=1, source_target_pairs={{0,4},{4,0},{8,12},{12,8},{16,20},{20,16},{24,28},{28,24},{32,36},... | collective-permute-start | bytes 1966088 | tf_op jit(solution)/shard_map/ppermute | solution.py:322
  64.6 26.3 %all-to-all-start = ((bf16[32,40,256]{2,1,0:T(8,128)(2,1)}), bf16[32,40,256]{2,1,0:T(8,128)(2,1)S(1)}, u32[]{:S(2)}, u32[]{:S(2)}) async-start(bf16[32,40,256]{2,1,0:T(8,128)(2,1)} %bitcast.5), calls=%async_computation | async-start | bytes 1310720 | tf_op jit(solution)/shard_map/all_to_all | solution.py:332
  74.2 23.1 %collective-permute-start.7 = (bf16[5,64,384]{2,1,0:T(8,128)(2,1)S(1)}, bf16[5,64,384]{2,1,0:T(8,128)(2,1)S(1)}, u32[]{:S(2)}, u32[]{:S(2)}) collective-permute-start(bf16[5,64,384]{2,1,0:T(8,128)(2,1)S(1)} %get-tuple-element.68), channel_id=1, source_target_pairs={{0,1},{1,0},{2,3},{3,2},{4,5},{5,4},{6,7},{7,6},{8,9},{9,8},{10,11... | collective-permute-start | bytes 737288 | tf_op jit(solution)/shard_map/ppermute | solution.py:262
  76.2 31.9 %collective-permute-start.8 = (bf16[5,64,384]{2,1,0:T(8,128)(2,1)S(1)}, bf16[5,64,384]{2,1,0:T(8,128)(2,1)S(1)}, u32[]{:S(2)}, u32[]{:S(2)}) collective-permute-start(bf16[5,64,384]{2,1,0:T(8,128)(2,1)S(1)} %get-tuple-element.69), channel_id=1, source_target_pairs={{0,2},{1,3},{2,0},{3,1},{4,6},{5,7},{6,4},{7,5},{8,10},{9,11},{10,... | collective-permute-start | bytes 737288 | tf_op jit(solution)/shard_map/ppermute | solution.py:262
  80.0 28.1 %collective-permute-start.9 = (bf16[5,64,384]{2,1,0:T(8,128)(2,1)S(1)}, bf16[5,64,384]{2,1,0:T(8,128)(2,1)S(1)}, u32[]{:S(2)}, u32[]{:S(2)}) collective-permute-start(bf16[5,64,384]{2,1,0:T(8,128)(2,1)S(1)} %get-tuple-element.70), channel_id=1, source_target_pairs={{0,3},{1,2},{2,1},{3,0},{4,7},{5,6},{6,5},{7,4},{8,11},{9,10},{10,... | collective-permute-start | bytes 737288 | tf_op jit(solution)/shard_map/ppermute | solution.py:262
  91.6 20.1 %collective-permute-start.11 = (bf16[80,384]{1,0:T(8,128)(2,1)S(1)}, bf16[80,384]{1,0:T(8,128)(2,1)S(1)}, u32[]{:S(2)}, u32[]{:S(2)}) collective-permute-start(bf16[80,384]{1,0:T(8,128)(2,1)S(1)} %get-tuple-element.76), channel_id=1, source_target_pairs={{0,1},{1,0},{2,3},{3,2},{4,5},{5,4},{6,7},{7,6},{8,9},{9,8},{10,11... | collective-permute-start | bytes 184328 | tf_op jit(solution)/shard_map/ppermute | solution.py:262
  91.7 20.0 %collective-permute-start.12 = (bf16[80,384]{1,0:T(8,128)(2,1)S(1)}, bf16[80,384]{1,0:T(8,128)(2,1)S(1)}, u32[]{:S(2)}, u32[]{:S(2)}) collective-permute-start(bf16[80,384]{1,0:T(8,128)(2,1)S(1)} %get-tuple-element.77), channel_id=1, source_target_pairs={{0,2},{1,3},{2,0},{3,1},{4,6},{5,7},{6,4},{7,5},{8,10},{9,11},{10,... | collective-permute-start | bytes 184328 | tf_op jit(solution)/shard_map/ppermute | solution.py:262
  97.3 14.3 %collective-permute-start.13 = (bf16[80,384]{1,0:T(8,128)(2,1)S(1)}, bf16[80,384]{1,0:T(8,128)(2,1)S(1)}, u32[]{:S(2)}, u32[]{:S(2)}) collective-permute-start(bf16[80,384]{1,0:T(8,128)(2,1)S(1)} %get-tuple-element.78), channel_id=1, source_target_pairs={{0,3},{1,2},{2,1},{3,0},{4,7},{5,6},{6,5},{7,4},{8,11},{9,10},{10,... | collective-permute-start | bytes 184328 | tf_op jit(solution)/shard_map/ppermute | solution.py:262

commit v3 on v2

--- a/solution.py
+++ b/solution.py
@@ -212,15 +212,20 @@
         o[LATE * OWN :, :] = ws[to]
 
 
-def unpack_body(scale, idx, a0, a1, a2, a3, b0, b1, b2, b3, y, g, w, sa, sb):
+def unpack_y_body(idx, a0, a1, a2, a3, y, sa):
+    for s, a in enumerate((a0, a1, a2, a3)):
+        sa[lax.bitwise_xor(idx[0], jnp.int32(s))] = a[:ROWS]
+    for r in range(ROWS):
+        y[r] = jnp.concatenate([sa[h, r][:, G_OFF : G_OFF + PART] for h in range(4)], axis=1)
+
+
+def unpack_g_body(scale, idx, a0, a1, a2, a3, b0, b1, b2, b3, g, w, sa, sb):
     for s, (a, b) in enumerate(((a0, b0), (a1, b1), (a2, b2), (a3, b3))):
         src = lax.bitwise_xor(idx[0], jnp.int32(s))
-        sa[src] = a[...]
+        sa[src] = a[ROWS:]
         sb[src] = b[...]
-    for r in range(ROWS):
-        y[r] = jnp.concatenate([sa[h, r][:, G_OFF : G_OFF + PART] for h in range(4)], axis=1)
     for r in range(ROWS - LATE):
-        g[r] = jnp.concatenate([sa[h, ROWS + r][:, :PART] for h in range(4)], axis=1)
+        g[r] = jnp.concatenate([sa[h, r][:, :PART] for h in range(4)], axis=1)
     for r in range(LATE):
         g[ROWS - LATE + r] = jnp.concatenate([sb[h, r * OWN : (r + 1) * OWN, :PART] for h in range(4)], axis=1)
     total = jnp.zeros((8, WIN), F32)
@@ -230,9 +235,7 @@
     total = total * scale
     for k in range(K):
         m, odd = divmod(k, 2)
-        for r in range(4):
-            row = 4 * odd + r
-            w[r, k : k + 1, :] = total[row : row + 1, m * OWN : (m + 1) * OWN]
+        w[k] = total[4 * odd : 4 * odd + 4, m * OWN : (m + 1) * OWN]
 
 
 def fold_core_body(idx, keep, got, out):
@@ -331,13 +334,18 @@
     groups = [[2 * q + core for q in range(32)] for core in range(2)]
     got = lax.all_to_all(half, "lat", 0, 0, axis_index_groups=groups, tiled=True)
     last = exchange(call(fold_lat_body, "fold_lat", [(late, BF)] * 4, 2, [pltpu.VMEM((4, 16, WIN), BF)])(idx, got, rest))
-    return call(
-        functools.partial(unpack_body, 1.0 / math.sqrt(64 * ROWS * J)),
-        "unpack",
-        [((ROWS, OWN, J), BF), ((ROWS, OWN, J), BF), ((4, K, OWN), F32)],
+    (y_field,) = call(
+        unpack_y_body, "unpack_y", [((ROWS, OWN, J), BF)], 4, [pltpu.VMEM((4, ROWS, OWN, WIN), BF)]
+    )(idx, *outs)
+    last, y_field = lax.optimization_barrier((last, y_field))
+    x_grad, w = call(
+        functools.partial(unpack_g_body, 1.0 / math.sqrt(64 * ROWS * J)),
+        "unpack_g",
+        [((ROWS, OWN, J), BF), ((K, 4, OWN), F32)],
         8,
-        [pltpu.VMEM((4, 2 * ROWS - LATE, OWN, WIN), BF), pltpu.VMEM((4,) + late, BF)],
+        [pltpu.VMEM((4, ROWS - LATE, OWN, WIN), BF), pltpu.VMEM((4,) + late, BF)],
     )(idx, *outs, *last)
+    return (y_field, x_grad, jnp.transpose(w, (1, 0, 2)))
 
 
 def solution(mesh):

time: 114 us -> 114 us (level)
  waiting for transfers between devices: 40.2 us -> 38.5 us
  Pallas kernels: 20.9 us -> 22.2 us
    ppermute x9, waiting for transfers between devices: 28 us -> 26.4 us  [exchange(): got = {s: lax.ppermute(parts[s], 'ch', swap_ch(s)) for s in (2, 1, 3)}]
    pallas_call x1 -> x2, Pallas kernels: 1.9 us -> 3.22 us  [the longest x1 1.63 us: local(): call(unpack_y_body, 'unpack_y', [((ROWS, OWN, J), BF)], 4, [pltpu.VMEM((4...]
  transfers between devices with their start and end apart: 15 -> 15, of which waited for: 7 -> 7; matrix products, arithmetic and copies ran while one was open for 1% -> 1% of each run, Pallas kernels for 13% -> 15%
where the time goes in v3:
time: 114 us; the launch traced here: 113 us
  starting transfers between devices  48.5 us (43%)
  waiting for transfers between devices  38.5 us (34%)
  Pallas kernels  22.2 us (19%)
  local copies, waits for them, and re-layouts  2.84 us (2%)
    ppermute x9, waiting for transfers between devices, exchange(): got = {s: lax.ppermute(parts[s], 'ch', swap_ch(s)) for s in (2, 1, 3)}  26.4 us
    ppermute x9, starting transfers between devices, exchange(): got = {s: lax.ppermute(parts[s], 'ch', swap_ch(s)) for s in (2, 1, 3)}  25.6 us
    all_to_all x1, waiting for transfers between devices, local(): lax.all_to_all(half, 'lat', 0, 0, axis_index_groups=groups, tiled=True)  10.9 us
    all_to_all x1, starting transfers between devices, local(): lax.all_to_all(half, 'lat', 0, 0, axis_index_groups=groups, tiled=True)  9.68 us
    pallas_call x1, Pallas kernels, local(): call(forward_body, 'forward', [((ROWS, C, WIN), BF), ((32, 40, C), F32),...  7.23 us
    ppermute x1, starting transfers between devices, local(): x_near = lax.ppermute(x_near, 'lat', to_near)  6.34 us
    pallas_call x1, Pallas kernels, local(): call(backward_body, 'backward', [((ROWS, WIN, C), F32), ((REACH, WIN, C),...  5.76 us
    ppermute x1, starting transfers between devices, local(): far = lax.ppermute(far, 'lat', to_far)  3.58 us
  transfers between devices with their start and end apart: 15, of which 7 were waited for; matrix products, arithmetic and copies ran while one was open for 1% of the time, Pallas kernels for 15%

profile of v3, /device:TPU:1, one launch (start us, length us, event | category | flops | bytes accessed | tf_op | source)
XLA Modules:
  0.0 113.3 jit_solution(7678536805195558659)
XLA Ops:
  0.7 0.1 pad_add_fusion.idx
  0.7 1.1 copy-done
  1.8 1.1 copy-done.1
  2.9 1.2 %pack.1 = (bf16[6,64,384]{2,1,0:T(8,128)(2,1)S(1)}, bf16[6,64,384]{2,1,0:T(8,128)(2,1)S(1)}, bf16[6,64,384]{2,1,0:T(8,128)(2,1)S(1)}, bf16[6,64,384]{2,1,0:T(8,128)(2,1)S(1)}) custom-call(s32[2]{0:T(128)S(1)} %pad_add_fusion.idx, bf16[3,64,1440]{2,1,0:T(8,128)(2,1)S(1)} %copy-done, bf16[3,64,1440]{2,1,0:T(8,128)(2,1)S(1)} %copy-done.1), custom_call_target="tpu_custom_call" | custom-call | bytes 1000000 | tf_op jit(solution)/shard_map/pack/pallas_call | solution.py:269
  4.1 3.9 %collective-permute-start = (bf16[6,64,384]{2,1,0:T(8,128)(2,1)S(1)}, bf16[6,64,384]{2,1,0:T(8,128)(2,1)S(1)}, u32[]{:S(2)}, u32[]{:S(2)}) collective-permute-start(bf16[6,64,384]{2,1,0:T(8,128)(2,1)S(1)} %get-tuple-element.49), channel_id=1, source_target_pairs={{0,1},{1,0},{2,3},{3,2},{4,5},{5,4},{6,7},{7,6},{8,9},{9,8},{10,11... | collective-permute-start | bytes 884744 | tf_op jit(solution)/shard_map/ppermute | solution.py:265
  8.0 5.1 %collective-permute-start.1 = (bf16[6,64,384]{2,1,0:T(8,128)(2,1)S(1)}, bf16[6,64,384]{2,1,0:T(8,128)(2,1)S(1)}, u32[]{:S(2)}, u32[]{:S(2)}) collective-permute-start(bf16[6,64,384]{2,1,0:T(8,128)(2,1)S(1)} %get-tuple-element.50), channel_id=1, source_target_pairs={{0,2},{1,3},{2,0},{3,1},{4,6},{5,7},{6,4},{7,5},{8,10},{9,11},{10,... | collective-permute-start | bytes 884744 | tf_op jit(solution)/shard_map/ppermute | solution.py:265
  13.1 0.0 collective-permute-start.2
  13.1 0.1 copy.12
  13.2 0.1 copy.13
  13.3 0.2 select_reduce_fusion
  13.5 0.2 rev.3
  13.7 0.0 copy-start.2
  13.8 0.1 reshape.50
  13.9 0.1 pad_bitcast_fusion
  14.0 0.1 reshape.51
  14.1 0.8 bands.1
  15.0 18.0 %collective-permute-done.p1.g1 = bf16[6,64,384]{2,1,0:T(8,128)(2,1)S(1)} collective-permute-done((bf16[6,64,384]{2,1,0:T(8,128)(2,1)S(1)}, bf16[6,64,384]{2,1,0:T(8,128)(2,1)S(1)}, u32[]{:S(2)}, u32[]{:S(2)}) %collective-permute-start) | collective-permute-done | bytes 294944 | tf_op jit(solution)/shard_map/ppermute | solution.py:265
  33.0 0.1 collective-permute-done.1.p2.g2
  33.2 0.6 collective-permute-done.2.p3.g3
  33.8 0.9 asm_x.1
  34.6 6.3 %collective-permute-start.3 = (bf16[2,400,256]{2,1,0:T(8,128)(2,1)S(1)}, bf16[2,400,256]{2,1,0:T(8,128)(2,1)S(1)}, u32[]{:S(2)}, u32[]{:S(2)}) collective-permute-start(bf16[2,400,256]{2,1,0:T(8,128)(2,1)S(1)} %get-tuple-element.59), channel_id=1, source_target_pairs={{0,4},{4,0},{8,12},{12,8},{16,20},{20,16},{24,28},{28,24},{32,36},... | collective-permute-start | bytes 1228808 | tf_op jit(solution)/shard_map/ppermute | solution.py:293
  41.0 3.1 %collective-permute-start.4 = (bf16[2,400,256]{2,1,0:T(8,128)(2,1)S(1)}, bf16[2,400,256]{2,1,0:T(8,128)(2,1)S(1)}, u32[]{:S(2)}, u32[]{:S(2)}) collective-permute-start(bf16[2,400,256]{2,1,0:T(8,128)(2,1)S(1)} %get-tuple-element.60), channel_id=1, source_target_pairs={{4,8},{8,4},{12,16},{16,12},{20,24},{24,20},{28,32},{32,28},{36,40... | collective-permute-start | bytes 1228808 | tf_op jit(solution)/shard_map/ppermute | solution.py:292
  44.1 5.8 %backward.1 = (f32[3,384,256]{2,1,0:T(8,128)S(1)}, bf16[2,384,256]{2,1,0:T(8,128)(2,1)S(1)}, bf16[2,384,256]{2,1,0:T(8,128)(2,1)S(1)}) custom-call(s32[2]{0:T(128)S(1)} %pad_add_fusion.idx, bf16[6,64,384]{2,1,0:T(8,128)(2,1)S(1)} %get-tuple-element.54.p0.g0, bf16[6,64,384]{2,1,0:T(8,128)(2,1)S(1)} %collective-permute-done.p1.g1, ...), custom_call_target="tpu_custom_call" | custom-call | flops 8000000000 | bytes 5000000 | tf_op jit(solution)/shard_map/backward/pallas_call | solution.py:296
  49.9 0.1 collective-permute-start.5
  50.0 3.6 %collective-permute-start.6 = (bf16[2,384,256]{2,1,0:T(8,128)(2,1)S(1)}, bf16[2,384,256]{2,1,0:T(8,128)(2,1)S(1)}, u32[]{:S(2)}, u32[]{:S(2)}) collective-permute-start(bf16[2,384,256]{2,1,0:T(8,128)(2,1)S(1)} %get-tuple-element.70), channel_id=1, source_target_pairs={{4,8},{8,4},{12,16},{16,12},{20,24},{24,20},{28,32},{32,28},{36,40... | collective-permute-start | bytes 1179656 | tf_op jit(solution)/shard_map/ppermute | solution.py:310
  53.6 0.0 collective-permute-done.3.near
  53.6 0.0 collective-permute-done.4.far
  53.6 7.2 %forward.1 = (bf16[3,256,384]{2,1,0:T(8,128)(2,1)S(1)}, f32[32,40,256]{2,1,0:T(8,128)S(1)}, bf16[1280,256]{1,0:T(8,128)(2,1)S(1)}) custom-call(s32[2]{0:T(128)S(1)} %pad_add_fusion.idx, bf16[3,400,256]{2,1,0:T(8,128)(2,1)S(1)} %get-tuple-element.58.x, bf16[2,400,256]{2,1,0:T(8,128)(2,1)S(1)} %collective-permute-done.3.near, ...), custom_call_target="tpu_custom_call" | custom-call | flops 8000000000 | bytes 9000000 | tf_op jit(solution)/shard_map/forward/pallas_call | solution.py:314
  60.8 0.0 collective-permute-done.6.far
  60.8 0.1 collective-permute-start.7
  60.9 0.8 join.1
  61.8 1.2 %collective-permute-done.7.got = bf16[1280,256]{1,0:T(8,128)(2,1)S(1)} collective-permute-done((bf16[1280,256]{1,0:T(8,128)(2,1)S(1)}, bf16[1280,256]{1,0:T(8,128)(2,1)S(1)}, u32[]{:S(2)}, u32[]{:S(2)}) %collective-permute-start.7) | collective-permute-done | bytes 655392 | tf_op jit(solution)/shard_map/ppermute | solution.py:325
  63.0 1.5 %fold_core.1 = bf16[1280,256]{1,0:T(8,128)(2,1)} custom-call(s32[2]{0:T(128)S(1)} %pad_add_fusion.idx, f32[1280,256]{1,0:T(8,128)S(1)} %bitcast.10, bf16[1280,256]{1,0:T(8,128)(2,1)S(1)} %collective-permute-done.7.got), custom_call_target="tpu_custom_call" | custom-call | bytes 1000000 | tf_op jit(solution)/shard_map/fold_core/pallas_call | solution.py:333
  64.6 9.7 %all-to-all-start = ((bf16[32,40,256]{2,1,0:T(8,128)(2,1)}), bf16[32,40,256]{2,1,0:T(8,128)(2,1)S(1)}, u32[]{:S(2)}, u32[]{:S(2)}) async-start(bf16[32,40,256]{2,1,0:T(8,128)(2,1)} %bitcast.5), calls=%async_computation | async-start | bytes 1310720 | tf_op jit(solution)/shard_map/all_to_all | solution.py:335
  74.2 2.0 %collective-permute-start.11 = (bf16[5,64,384]{2,1,0:T(8,128)(2,1)S(1)}, bf16[5,64,384]{2,1,0:T(8,128)(2,1)S(1)}, u32[]{:S(2)}, u32[]{:S(2)}) collective-permute-start(bf16[5,64,384]{2,1,0:T(8,128)(2,1)S(1)} %get-tuple-element.83), channel_id=1, source_target_pairs={{0,1},{1,0},{2,3},{3,2},{4,5},{5,4},{6,7},{7,6},{8,9},{9,8},{10,11... | collective-permute-start | bytes 737288 | tf_op jit(solution)/shard_map/ppermute | solution.py:265
  76.2 3.8 %collective-permute-start.12 = (bf16[5,64,384]{2,1,0:T(8,128)(2,1)S(1)}, bf16[5,64,384]{2,1,0:T(8,128)(2,1)S(1)}, u32[]{:S(2)}, u32[]{:S(2)}) collective-permute-start(bf16[5,64,384]{2,1,0:T(8,128)(2,1)S(1)} %get-tuple-element.84), channel_id=1, source_target_pairs={{0,2},{1,3},{2,0},{3,1},{4,6},{5,7},{6,4},{7,5},{8,10},{9,11},{10,... | collective-permute-start | bytes 737288 | tf_op jit(solution)/shard_map/ppermute | solution.py:265
  80.0 10.9 %all-to-all-done = bf16[32,40,256]{2,1,0:T(8,128)(2,1)S(1)} async-done(((bf16[32,40,256]{2,1,0:T(8,128)(2,1)}), bf16[32,40,256]{2,1,0:T(8,128)(2,1)S(1)}, u32[]{:S(2)}, u32[]{:S(2)}) %all-to-all-start) | async-done | bytes 655392 | tf_op jit(solution)/shard_map/all_to_all | solution.py:335
  90.9 0.7 fold_lat.1
  91.6 0.1 collective-permute-start.8
  91.7 5.6 %collective-permute-start.9 = (bf16[80,384]{1,0:T(8,128)(2,1)S(1)}, bf16[80,384]{1,0:T(8,128)(2,1)S(1)}, u32[]{:S(2)}, u32[]{:S(2)}) collective-permute-start(bf16[80,384]{1,0:T(8,128)(2,1)S(1)} %get-tuple-element.81), channel_id=1, source_target_pairs={{0,2},{1,3},{2,0},{3,1},{4,6},{5,7},{6,4},{7,5},{8,10},{9,11},{10,... | collective-permute-start | bytes 184328 | tf_op jit(solution)/shard_map/ppermute | solution.py:265
  97.3 5.1 %collective-permute-start.10 = (bf16[80,384]{1,0:T(8,128)(2,1)S(1)}, bf16[80,384]{1,0:T(8,128)(2,1)S(1)}, u32[]{:S(2)}, u32[]{:S(2)}) collective-permute-start(bf16[80,384]{1,0:T(8,128)(2,1)S(1)} %get-tuple-element.82), channel_id=1, source_target_pairs={{0,3},{1,2},{2,1},{3,0},{4,7},{5,6},{6,5},{7,4},{8,11},{9,10},{10,... | collective-permute-start | bytes 184328 | tf_op jit(solution)/shard_map/ppermute | solution.py:265
  102.5 5.7 %collective-permute-done.12.a2 = bf16[5,64,384]{2,1,0:T(8,128)(2,1)S(1)} collective-permute-done((bf16[5,64,384]{2,1,0:T(8,128)(2,1)S(1)}, bf16[5,64,384]{2,1,0:T(8,128)(2,1)S(1)}, u32[]{:S(2)}, u32[]{:S(2)}) %collective-permute-start.12) | collective-permute-done | bytes 245792 | tf_op jit(solution)/shard_map/ppermute | solution.py:265
  108.1 0.0 collective-permute-done.13.a3
  108.1 1.6 %unpack_y.1 = bf16[3,64,1440]{2,1,0:T(8,128)(2,1)} custom-call(s32[2]{0:T(128)S(1)} %pad_add_fusion.idx, bf16[5,64,384]{2,1,0:T(8,128)(2,1)S(1)} %get-tuple-element.76.a0, bf16[5,64,384]{2,1,0:T(8,128)(2,1)S(1)} %collective-permute-done.11.a1, bf16[5,64,384]{2,1,0:T(8,128)(2,1)S(1)} %collective-permute-done.12.a2, ...), custom_call_target="tpu_custom_call" | custom-call | bytes 1000000 | tf_op jit(solution)/shard_map/unpack_y/pallas_call | solution.py:337
  109.7 1.9 %collective-permute-done.8.b1 = bf16[80,384]{1,0:T(8,128)(2,1)S(1)} collective-permute-done((bf16[80,384]{1,0:T(8,128)(2,1)S(1)}, bf16[80,384]{1,0:T(8,128)(2,1)S(1)}, u32[]{:S(2)}, u32[]{:S(2)}) %collective-permute-start.8) | collective-permute-done | bytes 61472 | tf_op jit(solution)/shard_map/ppermute | solution.py:265
  111.7 0.0 collective-permute-done.9.b2
  111.7 0.0 collective-permute-done.10.b3
  111.7 1.6 %unpack_g.1 = (bf16[3,64,1440]{2,1,0:T(8,128)(2,1)}, f32[9,4,64]{2,1,0:T(4,128)}) custom-call(s32[2]{0:T(128)S(1)} %pad_add_fusion.idx, bf16[5,64,384]{2,1,0:T(8,128)(2,1)S(1)} %get-tuple-element.76.a0, bf16[5,64,384]{2,1,0:T(8,128)(2,1)S(1)} %collective-permute-done.11.a1, bf16[5,64,384]{2,1,0:T(8,128)(2,1)S(1)} %collective-permute-done.12.a2, ...), custom_call_target="tpu_custom_call" | custom-call | bytes 1000000 | tf_op jit(solution)/shard_map/unpack_g/pallas_call | solution.py:341
  (20 shorter events, 0.1 us)
Async XLA Ops:
  0.6 12.4 %copy-start.4 = (s32[3,5]{1,0:T(4,128)S(1)}, s32[3,5]{1,0:T(4,128)}, u32[]{:S(2)}) copy-start(s32[3,5]{1,0:T(4,128)} %param.7) | copy-start | bytes 184
  0.7 1.1 copy-start
  1.8 1.1 copy-start.1
  2.9 10.5 %copy-start.3 = (bf16[3,5,9,16]{3,0,2,1:T(4,128)(2,1)S(1)}, bf16[3,5,9,16]{3,0,2,1:T(4,128)(2,1)}, u32[]{:S(2)}) copy-start(bf16[3,5,9,16]{3,0,2,1:T(4,128)(2,1)} %param.8) | copy-start | bytes 12964
  4.1 29.0 %collective-permute-start = (bf16[6,64,384]{2,1,0:T(8,128)(2,1)S(1)}, bf16[6,64,384]{2,1,0:T(8,128)(2,1)S(1)}, u32[]{:S(2)}, u32[]{:S(2)}) collective-permute-start(bf16[6,64,384]{2,1,0:T(8,128)(2,1)S(1)} %get-tuple-element.49), channel_id=1, source_target_pairs={{0,1},{1,0},{2,3},{3,2},{4,5},{5,4},{6,7},{7,6},{8,9},{9,8},{10,11... | collective-permute-start | bytes 884744 | tf_op jit(solution)/shard_map/ppermute | solution.py:265
  8.0 25.2 %collective-permute-start.1 = (bf16[6,64,384]{2,1,0:T(8,128)(2,1)S(1)}, bf16[6,64,384]{2,1,0:T(8,128)(2,1)S(1)}, u32[]{:S(2)}, u32[]{:S(2)}) collective-permute-start(bf16[6,64,384]{2,1,0:T(8,128)(2,1)S(1)} %get-tuple-element.50), channel_id=1, source_target_pairs={{0,2},{1,3},{2,0},{3,1},{4,6},{5,7},{6,4},{7,5},{8,10},{9,11},{10,... | collective-permute-start | bytes 884744 | tf_op jit(solution)/shard_map/ppermute | solution.py:265
  13.1 20.7 %collective-permute-start.2 = (bf16[6,64,384]{2,1,0:T(8,128)(2,1)S(1)}, bf16[6,64,384]{2,1,0:T(8,128)(2,1)S(1)}, u32[]{:S(2)}, u32[]{:S(2)}) collective-permute-start(bf16[6,64,384]{2,1,0:T(8,128)(2,1)S(1)} %get-tuple-element.51), channel_id=1, source_target_pairs={{0,3},{1,2},{2,1},{3,0},{4,7},{5,6},{6,5},{7,4},{8,11},{9,10},{10,... | collective-permute-start | bytes 884744 | tf_op jit(solution)/shard_map/ppermute | solution.py:265
  13.7 30.4 %copy-start.2 = (bf16[9,256,256]{2,1,0:T(8,128)(2,1)S(1)}, bf16[9,256,256]{2,1,0:T(8,128)(2,1)}, u32[]{:S(2)}) copy-start(bf16[9,256,256]{2,1,0:T(8,128)(2,1)} %param.9) | copy-start | bytes 3538948
  34.6 18.9 %collective-permute-start.3 = (bf16[2,400,256]{2,1,0:T(8,128)(2,1)S(1)}, bf16[2,400,256]{2,1,0:T(8,128)(2,1)S(1)}, u32[]{:S(2)}, u32[]{:S(2)}) collective-permute-start(bf16[2,400,256]{2,1,0:T(8,128)(2,1)S(1)} %get-tuple-element.59), channel_id=1, source_target_pairs={{0,4},{4,0},{8,12},{12,8},{16,20},{20,16},{24,28},{28,24},{32,36},... | collective-permute-start | bytes 1228808 | tf_op jit(solution)/shard_map/ppermute | solution.py:293
  41.0 12.6 %collective-permute-start.4 = (bf16[2,400,256]{2,1,0:T(8,128)(2,1)S(1)}, bf16[2,400,256]{2,1,0:T(8,128)(2,1)S(1)}, u32[]{:S(2)}, u32[]{:S(2)}) collective-permute-start(bf16[2,400,256]{2,1,0:T(8,128)(2,1)S(1)} %get-tuple-element.60), channel_id=1, source_target_pairs={{4,8},{8,4},{12,16},{16,12},{20,24},{24,20},{28,32},{32,28},{36,40... | collective-permute-start | bytes 1228808 | tf_op jit(solution)/shard_map/ppermute | solution.py:292
  49.9 10.9 %collective-permute-start.5 = (bf16[2,384,256]{2,1,0:T(8,128)(2,1)S(1)}, bf16[2,384,256]{2,1,0:T(8,128)(2,1)S(1)}, u32[]{:S(2)}, u32[]{:S(2)}) collective-permute-start(bf16[2,384,256]{2,1,0:T(8,128)(2,1)S(1)} %get-tuple-element.69), channel_id=1, source_target_pairs={{0,4},{4,0},{8,12},{12,8},{16,20},{20,16},{24,28},{28,24},{32,36},... | collective-permute-start | bytes 1179656 | tf_op jit(solution)/shard_map/ppermute | solution.py:311
  50.0 10.9 %collective-permute-start.6 = (bf16[2,384,256]{2,1,0:T(8,128)(2,1)S(1)}, bf16[2,384,256]{2,1,0:T(8,128)(2,1)S(1)}, u32[]{:S(2)}, u32[]{:S(2)}) collective-permute-start(bf16[2,384,256]{2,1,0:T(8,128)(2,1)S(1)} %get-tuple-element.70), channel_id=1, source_target_pairs={{4,8},{8,4},{12,16},{16,12},{20,24},{24,20},{28,32},{32,28},{36,40... | collective-permute-start | bytes 1179656 | tf_op jit(solution)/shard_map/ppermute | solution.py:310
  60.8 2.2 %collective-permute-start.7 = (bf16[1280,256]{1,0:T(8,128)(2,1)S(1)}, bf16[1280,256]{1,0:T(8,128)(2,1)S(1)}, u32[]{:S(2)}, u32[]{:S(2)}) collective-permute-start(bf16[1280,256]{1,0:T(8,128)(2,1)S(1)} %get-tuple-element.71), channel_id=1, source_target_pairs={{0,4},{4,0},{8,12},{12,8},{16,20},{20,16},{24,28},{28,24},{32,36},... | collective-permute-start | bytes 1966088 | tf_op jit(solution)/shard_map/ppermute | solution.py:325
  64.6 26.3 %all-to-all-start = ((bf16[32,40,256]{2,1,0:T(8,128)(2,1)}), bf16[32,40,256]{2,1,0:T(8,128)(2,1)S(1)}, u32[]{:S(2)}, u32[]{:S(2)}) async-start(bf16[32,40,256]{2,1,0:T(8,128)(2,1)} %bitcast.5), calls=%async_computation | async-start | bytes 1310720 | tf_op jit(solution)/shard_map/all_to_all | solution.py:335
  74.2 23.1 %collective-permute-start.11 = (bf16[5,64,384]{2,1,0:T(8,128)(2,1)S(1)}, bf16[5,64,384]{2,1,0:T(8,128)(2,1)S(1)}, u32[]{:S(2)}, u32[]{:S(2)}) collective-permute-start(bf16[5,64,384]{2,1,0:T(8,128)(2,1)S(1)} %get-tuple-element.83), channel_id=1, source_target_pairs={{0,1},{1,0},{2,3},{3,2},{4,5},{5,4},{6,7},{7,6},{8,9},{9,8},{10,11... | collective-permute-start | bytes 737288 | tf_op jit(solution)/shard_map/ppermute | solution.py:265
  76.2 31.9 %collective-permute-start.12 = (bf16[5,64,384]{2,1,0:T(8,128)(2,1)S(1)}, bf16[5,64,384]{2,1,0:T(8,128)(2,1)S(1)}, u32[]{:S(2)}, u32[]{:S(2)}) collective-permute-start(bf16[5,64,384]{2,1,0:T(8,128)(2,1)S(1)} %get-tuple-element.84), channel_id=1, source_target_pairs={{0,2},{1,3},{2,0},{3,1},{4,6},{5,7},{6,4},{7,5},{8,10},{9,11},{10,... | collective-permute-start | bytes 737288 | tf_op jit(solution)/shard_map/ppermute | solution.py:265
  80.0 28.1 %collective-permute-start.13 = (bf16[5,64,384]{2,1,0:T(8,128)(2,1)S(1)}, bf16[5,64,384]{2,1,0:T(8,128)(2,1)S(1)}, u32[]{:S(2)}, u32[]{:S(2)}) collective-permute-start(bf16[5,64,384]{2,1,0:T(8,128)(2,1)S(1)} %get-tuple-element.85), channel_id=1, source_target_pairs={{0,3},{1,2},{2,1},{3,0},{4,7},{5,6},{6,5},{7,4},{8,11},{9,10},{10,... | collective-permute-start | bytes 737288 | tf_op jit(solution)/shard_map/ppermute | solution.py:265
  91.6 20.1 %collective-permute-start.8 = (bf16[80,384]{1,0:T(8,128)(2,1)S(1)}, bf16[80,384]{1,0:T(8,128)(2,1)S(1)}, u32[]{:S(2)}, u32[]{:S(2)}) collective-permute-start(bf16[80,384]{1,0:T(8,128)(2,1)S(1)} %get-tuple-element.80), channel_id=1, source_target_pairs={{0,1},{1,0},{2,3},{3,2},{4,5},{5,4},{6,7},{7,6},{8,9},{9,8},{10,11... | collective-permute-start | bytes 184328 | tf_op jit(solution)/shard_map/ppermute | solution.py:265
  91.7 20.0 %collective-permute-start.9 = (bf16[80,384]{1,0:T(8,128)(2,1)S(1)}, bf16[80,384]{1,0:T(8,128)(2,1)S(1)}, u32[]{:S(2)}, u32[]{:S(2)}) collective-permute-start(bf16[80,384]{1,0:T(8,128)(2,1)S(1)} %get-tuple-element.81), channel_id=1, source_target_pairs={{0,2},{1,3},{2,0},{3,1},{4,6},{5,7},{6,4},{7,5},{8,10},{9,11},{10,... | collective-permute-start | bytes 184328 | tf_op jit(solution)/shard_map/ppermute | solution.py:265
  97.3 14.3 %collective-permute-start.10 = (bf16[80,384]{1,0:T(8,128)(2,1)S(1)}, bf16[80,384]{1,0:T(8,128)(2,1)S(1)}, u32[]{:S(2)}, u32[]{:S(2)}) collective-permute-start(bf16[80,384]{1,0:T(8,128)(2,1)S(1)} %get-tuple-element.82), channel_id=1, source_target_pairs={{0,3},{1,2},{2,1},{3,0},{4,7},{5,6},{6,5},{7,4},{8,11},{9,10},{10,... | collective-permute-start | bytes 184328 | tf_op jit(solution)/shard_map/ppermute | solution.py:265

commit v4 on v3

--- a/solution.py
+++ b/solution.py
@@ -57,12 +57,12 @@
                 w = v[:, a : a + WIN]
             win[h, r] = w
     for s, o in enumerate((o0, o1, o2, o3)):
-        o[...] = win[lax.bitwise_xor(idx[0], jnp.int32(s))]
+        o[...] = win[lax.rem(idx[0] + s, 4)]
 
 
 def gather_parts(ch, refs, first, scr):
     for s, ref in enumerate(refs):
-        src = lax.bitwise_xor(ch, jnp.int32(s))
+        src = lax.rem(ch - s + 4, 4)
         scr[:, pl.ds(pl.multiple_of(src * OWN, OWN), OWN), :] = ref[first : first + ROWS]
 
 
@@ -192,7 +192,7 @@
         else:
             rest[r - (ROWS - LATE)] = v.T.astype(BF)
     for s, o in enumerate((o0, o1, o2, o3)):
-        to = lax.bitwise_xor(idx[0], jnp.int32(s))
+        to = lax.rem(idx[0] + s, 4)
         at = pl.ds(pl.multiple_of(to * OWN, OWN), OWN)
         o[:ROWS] = yt[:, at, :]
         o[ROWS:] = scr[:, at, :]
@@ -206,7 +206,7 @@
         high = v.astype(BF).astype(F32)
         ws[h] = jnp.concatenate([high, v - high], axis=0).astype(BF)
     for s, o in enumerate((o0, o1, o2, o3)):
-        to = lax.bitwise_xor(idx[0], jnp.int32(s))
+        to = lax.rem(idx[0] + s, 4)
         for r in range(LATE):
             o[r * OWN : (r + 1) * OWN, :] = rest[r, pl.ds(pl.multiple_of(to * OWN, OWN), OWN), :]
         o[LATE * OWN :, :] = ws[to]
@@ -214,14 +214,14 @@
 
 def unpack_y_body(idx, a0, a1, a2, a3, y, sa):
     for s, a in enumerate((a0, a1, a2, a3)):
-        sa[lax.bitwise_xor(idx[0], jnp.int32(s))] = a[:ROWS]
+        sa[lax.rem(idx[0] - s + 4, 4)] = a[:ROWS]
     for r in range(ROWS):
         y[r] = jnp.concatenate([sa[h, r][:, G_OFF : G_OFF + PART] for h in range(4)], axis=1)
 
 
 def unpack_g_body(scale, idx, a0, a1, a2, a3, b0, b1, b2, b3, g, w, sa, sb):
     for s, (a, b) in enumerate(((a0, b0), (a1, b1), (a2, b2), (a3, b3))):
-        src = lax.bitwise_xor(idx[0], jnp.int32(s))
+        src = lax.rem(idx[0] - s + 4, 4)
         sa[src] = a[ROWS:]
         sb[src] = b[...]
     for r in range(ROWS - LATE):
@@ -242,8 +242,8 @@
     out[...] = (keep[...] + got[...].astype(F32)).astype(BF)
 
 
-def swap_ch(mask):
-    return [(i, i ^ mask) for i in range(4)]
+def ring_ch(step):
+    return [(i, (i + step) % 4) for i in range(4)]
 
 
 def swap_lat():
@@ -262,7 +262,7 @@
     pair = ((2 * ROWS, OWN, WIN), BF)
 
     def exchange(parts):
-        got = {s: lax.ppermute(parts[s], "ch", swap_ch(s)) for s in (2, 1, 3)}
+        got = {s: lax.ppermute(parts[s], "ch", ring_ch(s)) for s in (2, 1, 3)}
         return [parts[0], got[1], got[2], got[3]]
 
     parts = exchange(

time: 114 us -> 113 us (level)
    all_to_all x1, waiting for transfers between devices: 10.9 us -> 4.4 us  [local(): lax.all_to_all(half, 'lat', 0, 0, axis_index_groups=groups, tiled=True)]
    ppermute x9, starting transfers between devices: 25.6 us -> 31.6 us  [exchange(): got = {s: lax.ppermute(parts[s], 'ch', ring_ch(s)) for s in (2, 1, 3)}]
    ppermute x9, waiting for transfers between devices: 26.4 us -> 32.2 us  [exchange(): got = {s: lax.ppermute(parts[s], 'ch', ring_ch(s)) for s in (2, 1, 3)}]
    ppermute x1, starting transfers between devices: 6.34 us -> 0.57 us  [local(): x_near = lax.ppermute(x_near, 'lat', to_near)]
  transfers between devices with their start and end apart: 15 -> 15, of which waited for: 7 -> 9; matrix products, arithmetic and copies ran while one was open for 1% -> 1% of each run, Pallas kernels for 15% -> 15%
where the time goes in v4:
time: 113 us
  starting transfers between devices  48.8 us (43%)
  waiting for transfers between devices  37.8 us (33%)
  Pallas kernels  22.3 us (20%)
  local copies, waits for them, and re-layouts  2.84 us (3%)
    ppermute x9, waiting for transfers between devices, exchange(): got = {s: lax.ppermute(parts[s], 'ch', ring_ch(s)) for s in (2, 1, 3)}  32.2 us
    ppermute x9, starting transfers between devices, exchange(): got = {s: lax.ppermute(parts[s], 'ch', ring_ch(s)) for s in (2, 1, 3)}  31.6 us
    all_to_all x1, starting transfers between devices, local(): lax.all_to_all(half, 'lat', 0, 0, axis_index_groups=groups, tiled=True)  9.69 us
    pallas_call x1, Pallas kernels, local(): call(forward_body, 'forward', [((ROWS, C, WIN), BF), ((32, 40, C), F32),...  7.21 us
    pallas_call x1, Pallas kernels, local(): call(backward_body, 'backward', [((ROWS, WIN, C), F32), ((REACH, WIN, C),...  5.74 us
    all_to_all x1, waiting for transfers between devices, local(): lax.all_to_all(half, 'lat', 0, 0, axis_index_groups=groups, tiled=True)  4.4 us
    ppermute x1, starting transfers between devices, local(): far = lax.ppermute(far, 'lat', to_far)  3.57 us
    ppermute x1, starting transfers between devices, local(): x_far = lax.ppermute(x_far, 'lat', to_far)  3.1 us
  transfers between devices with their start and end apart: 15, of which 9 were waited for; matrix products, arithmetic and copies ran while one was open for 1% of the time, Pallas kernels for 15%

profile of v4, /device:TPU:1, one launch (start us, length us, event | category | flops | bytes accessed | tf_op | source)
XLA Modules:
  0.0 112.9 jit_solution(15162081628605778883)
XLA Ops:
  0.7 0.1 pad_add_fusion.idx
  0.7 1.1 copy-done
  1.8 1.1 copy-done.1
  2.9 1.2 %pack.1 = (bf16[6,64,384]{2,1,0:T(8,128)(2,1)S(1)}, bf16[6,64,384]{2,1,0:T(8,128)(2,1)S(1)}, bf16[6,64,384]{2,1,0:T(8,128)(2,1)S(1)}, bf16[6,64,384]{2,1,0:T(8,128)(2,1)S(1)}) custom-call(s32[2]{0:T(128)S(1)} %pad_add_fusion.idx, bf16[3,64,1440]{2,1,0:T(8,128)(2,1)S(1)} %copy-done, bf16[3,64,1440]{2,1,0:T(8,128)(2,1)S(1)} %copy-done.1), custom_call_target="tpu_custom_call" | custom-call | bytes 1000000 | tf_op jit(solution)/shard_map/pack/pallas_call | solution.py:269
  4.0 3.9 %collective-permute-start = (bf16[6,64,384]{2,1,0:T(8,128)(2,1)S(1)}, bf16[6,64,384]{2,1,0:T(8,128)(2,1)S(1)}, u32[]{:S(2)}, u32[]{:S(2)}) collective-permute-start(bf16[6,64,384]{2,1,0:T(8,128)(2,1)S(1)} %get-tuple-element.49), channel_id=1, source_target_pairs={{0,1},{1,2},{2,3},{3,0},{4,5},{5,6},{6,7},{7,4},{8,9},{9,10},{10,1... | collective-permute-start | bytes 884744 | tf_op jit(solution)/shard_map/ppermute | solution.py:265
  7.9 5.1 %collective-permute-start.1 = (bf16[6,64,384]{2,1,0:T(8,128)(2,1)S(1)}, bf16[6,64,384]{2,1,0:T(8,128)(2,1)S(1)}, u32[]{:S(2)}, u32[]{:S(2)}) collective-permute-start(bf16[6,64,384]{2,1,0:T(8,128)(2,1)S(1)} %get-tuple-element.50), channel_id=1, source_target_pairs={{0,2},{1,3},{2,0},{3,1},{4,6},{5,7},{6,4},{7,5},{8,10},{9,11},{10,... | collective-permute-start | bytes 884744 | tf_op jit(solution)/shard_map/ppermute | solution.py:265
  13.1 2.4 %collective-permute-start.2 = (bf16[6,64,384]{2,1,0:T(8,128)(2,1)S(1)}, bf16[6,64,384]{2,1,0:T(8,128)(2,1)S(1)}, u32[]{:S(2)}, u32[]{:S(2)}) collective-permute-start(bf16[6,64,384]{2,1,0:T(8,128)(2,1)S(1)} %get-tuple-element.51), channel_id=1, source_target_pairs={{0,3},{1,0},{2,1},{3,2},{4,7},{5,4},{6,5},{7,6},{8,11},{9,8},{10,9... | collective-permute-start | bytes 884744 | tf_op jit(solution)/shard_map/ppermute | solution.py:265
  15.4 0.1 copy.12
  15.5 0.1 copy.13
  15.7 0.2 select_reduce_fusion
  15.9 0.2 rev.3
  16.1 0.0 copy-start.2
  16.1 0.1 reshape.50
  16.2 0.1 pad_bitcast_fusion
  16.4 0.1 reshape.51
  16.5 0.8 bands.1
  17.3 2.4 %collective-permute-done.p1.g1 = bf16[6,64,384]{2,1,0:T(8,128)(2,1)S(1)} collective-permute-done((bf16[6,64,384]{2,1,0:T(8,128)(2,1)S(1)}, bf16[6,64,384]{2,1,0:T(8,128)(2,1)S(1)}, u32[]{:S(2)}, u32[]{:S(2)}) %collective-permute-start) | collective-permute-done | bytes 294944 | tf_op jit(solution)/shard_map/ppermute | solution.py:265
  19.7 10.5 %collective-permute-done.1.p2.g2 = bf16[6,64,384]{2,1,0:T(8,128)(2,1)S(1)} collective-permute-done((bf16[6,64,384]{2,1,0:T(8,128)(2,1)S(1)}, bf16[6,64,384]{2,1,0:T(8,128)(2,1)S(1)}, u32[]{:S(2)}, u32[]{:S(2)}) %collective-permute-start.1) | collective-permute-done | bytes 294944 | tf_op jit(solution)/shard_map/ppermute | solution.py:265
  30.2 9.9 %collective-permute-done.2.p3.g3 = bf16[6,64,384]{2,1,0:T(8,128)(2,1)S(1)} collective-permute-done((bf16[6,64,384]{2,1,0:T(8,128)(2,1)S(1)}, bf16[6,64,384]{2,1,0:T(8,128)(2,1)S(1)}, u32[]{:S(2)}, u32[]{:S(2)}) %collective-permute-start.2) | collective-permute-done | bytes 294944 | tf_op jit(solution)/shard_map/ppermute | solution.py:265
  40.1 0.9 asm_x.1
  41.0 0.6 collective-permute-start.3
  41.6 3.1 %collective-permute-start.4 = (bf16[2,400,256]{2,1,0:T(8,128)(2,1)S(1)}, bf16[2,400,256]{2,1,0:T(8,128)(2,1)S(1)}, u32[]{:S(2)}, u32[]{:S(2)}) collective-permute-start(bf16[2,400,256]{2,1,0:T(8,128)(2,1)S(1)} %get-tuple-element.60), channel_id=1, source_target_pairs={{4,8},{8,4},{12,16},{16,12},{20,24},{24,20},{28,32},{32,28},{36,40... | collective-permute-start | bytes 1228808 | tf_op jit(solution)/shard_map/ppermute | solution.py:292
  44.7 5.7 %backward.1 = (f32[3,384,256]{2,1,0:T(8,128)S(1)}, bf16[2,384,256]{2,1,0:T(8,128)(2,1)S(1)}, bf16[2,384,256]{2,1,0:T(8,128)(2,1)S(1)}) custom-call(s32[2]{0:T(128)S(1)} %pad_add_fusion.idx, bf16[6,64,384]{2,1,0:T(8,128)(2,1)S(1)} %get-tuple-element.54.p0.g0, bf16[6,64,384]{2,1,0:T(8,128)(2,1)S(1)} %collective-permute-done.p1.g1, ...), custom_call_target="tpu_custom_call" | custom-call | flops 8000000000 | bytes 5000000 | tf_op jit(solution)/shard_map/backward/pallas_call | solution.py:296
  50.4 0.1 collective-permute-start.5
  50.5 3.6 %collective-permute-start.6 = (bf16[2,384,256]{2,1,0:T(8,128)(2,1)S(1)}, bf16[2,384,256]{2,1,0:T(8,128)(2,1)S(1)}, u32[]{:S(2)}, u32[]{:S(2)}) collective-permute-start(bf16[2,384,256]{2,1,0:T(8,128)(2,1)S(1)} %get-tuple-element.70), channel_id=1, source_target_pairs={{4,8},{8,4},{12,16},{16,12},{20,24},{24,20},{28,32},{32,28},{36,40... | collective-permute-start | bytes 1179656 | tf_op jit(solution)/shard_map/ppermute | solution.py:310
  54.1 0.0 collective-permute-done.3.near
  54.1 0.0 collective-permute-done.4.far
  54.2 7.2 %forward.1 = (bf16[3,256,384]{2,1,0:T(8,128)(2,1)S(1)}, f32[32,40,256]{2,1,0:T(8,128)S(1)}, bf16[1280,256]{1,0:T(8,128)(2,1)S(1)}) custom-call(s32[2]{0:T(128)S(1)} %pad_add_fusion.idx, bf16[3,400,256]{2,1,0:T(8,128)(2,1)S(1)} %get-tuple-element.58.x, bf16[2,400,256]{2,1,0:T(8,128)(2,1)S(1)} %collective-permute-done.3.near, ...), custom_call_target="tpu_custom_call" | custom-call | flops 8000000000 | bytes 9000000 | tf_op jit(solution)/shard_map/forward/pallas_call | solution.py:314
  61.4 0.0 collective-permute-done.5.near
  61.4 0.1 collective-permute-start.7
  61.5 0.9 join.1
  62.4 1.1 %collective-permute-done.7.got = bf16[1280,256]{1,0:T(8,128)(2,1)S(1)} collective-permute-done((bf16[1280,256]{1,0:T(8,128)(2,1)S(1)}, bf16[1280,256]{1,0:T(8,128)(2,1)S(1)}, u32[]{:S(2)}, u32[]{:S(2)}) %collective-permute-start.7) | collective-permute-done | bytes 655392 | tf_op jit(solution)/shard_map/ppermute | solution.py:325
  63.6 1.5 %fold_core.1 = bf16[1280,256]{1,0:T(8,128)(2,1)} custom-call(s32[2]{0:T(128)S(1)} %pad_add_fusion.idx, f32[1280,256]{1,0:T(8,128)S(1)} %bitcast.10, bf16[1280,256]{1,0:T(8,128)(2,1)S(1)} %collective-permute-done.7.got), custom_call_target="tpu_custom_call" | custom-call | bytes 1000000 | tf_op jit(solution)/shard_map/fold_core/pallas_call | solution.py:333
  65.1 9.7 %all-to-all-start = ((bf16[32,40,256]{2,1,0:T(8,128)(2,1)}), bf16[32,40,256]{2,1,0:T(8,128)(2,1)S(1)}, u32[]{:S(2)}, u32[]{:S(2)}) async-start(bf16[32,40,256]{2,1,0:T(8,128)(2,1)} %bitcast.5), calls=%async_computation | async-start | bytes 1310720 | tf_op jit(solution)/shard_map/all_to_all | solution.py:335
  74.8 1.5 %collective-permute-start.11 = (bf16[5,64,384]{2,1,0:T(8,128)(2,1)S(1)}, bf16[5,64,384]{2,1,0:T(8,128)(2,1)S(1)}, u32[]{:S(2)}, u32[]{:S(2)}) collective-permute-start(bf16[5,64,384]{2,1,0:T(8,128)(2,1)S(1)} %get-tuple-element.83), channel_id=1, source_target_pairs={{0,1},{1,2},{2,3},{3,0},{4,5},{5,6},{6,7},{7,4},{8,9},{9,10},{10,1... | collective-permute-start | bytes 737288 | tf_op jit(solution)/shard_map/ppermute | solution.py:265
  76.3 4.1 %collective-permute-start.12 = (bf16[5,64,384]{2,1,0:T(8,128)(2,1)S(1)}, bf16[5,64,384]{2,1,0:T(8,128)(2,1)S(1)}, u32[]{:S(2)}, u32[]{:S(2)}) collective-permute-start(bf16[5,64,384]{2,1,0:T(8,128)(2,1)S(1)} %get-tuple-element.84), channel_id=1, source_target_pairs={{0,2},{1,3},{2,0},{3,1},{4,6},{5,7},{6,4},{7,5},{8,10},{9,11},{10,... | collective-permute-start | bytes 737288 | tf_op jit(solution)/shard_map/ppermute | solution.py:265
  80.4 2.2 %collective-permute-start.13 = (bf16[5,64,384]{2,1,0:T(8,128)(2,1)S(1)}, bf16[5,64,384]{2,1,0:T(8,128)(2,1)S(1)}, u32[]{:S(2)}, u32[]{:S(2)}) collective-permute-start(bf16[5,64,384]{2,1,0:T(8,128)(2,1)S(1)} %get-tuple-element.85), channel_id=1, source_target_pairs={{0,3},{1,0},{2,1},{3,2},{4,7},{5,4},{6,5},{7,6},{8,11},{9,8},{10,9... | collective-permute-start | bytes 737288 | tf_op jit(solution)/shard_map/ppermute | solution.py:265
  82.6 4.4 %all-to-all-done = bf16[32,40,256]{2,1,0:T(8,128)(2,1)S(1)} async-done(((bf16[32,40,256]{2,1,0:T(8,128)(2,1)}), bf16[32,40,256]{2,1,0:T(8,128)(2,1)S(1)}, u32[]{:S(2)}, u32[]{:S(2)}) %all-to-all-start) | async-done | bytes 655392 | tf_op jit(solution)/shard_map/all_to_all | solution.py:335
  87.0 0.7 fold_lat.1
  87.7 1.3 %collective-permute-start.8 = (bf16[80,384]{1,0:T(8,128)(2,1)S(1)}, bf16[80,384]{1,0:T(8,128)(2,1)S(1)}, u32[]{:S(2)}, u32[]{:S(2)}) collective-permute-start(bf16[80,384]{1,0:T(8,128)(2,1)S(1)} %get-tuple-element.80), channel_id=1, source_target_pairs={{0,1},{1,2},{2,3},{3,0},{4,5},{5,6},{6,7},{7,4},{8,9},{9,10},{10,1... | collective-permute-start | bytes 184328 | tf_op jit(solution)/shard_map/ppermute | solution.py:265
  89.1 7.6 %collective-permute-start.9 = (bf16[80,384]{1,0:T(8,128)(2,1)S(1)}, bf16[80,384]{1,0:T(8,128)(2,1)S(1)}, u32[]{:S(2)}, u32[]{:S(2)}) collective-permute-start(bf16[80,384]{1,0:T(8,128)(2,1)S(1)} %get-tuple-element.81), channel_id=1, source_target_pairs={{0,2},{1,3},{2,0},{3,1},{4,6},{5,7},{6,4},{7,5},{8,10},{9,11},{10,... | collective-permute-start | bytes 184328 | tf_op jit(solution)/shard_map/ppermute | solution.py:265
  96.7 3.5 %collective-permute-start.10 = (bf16[80,384]{1,0:T(8,128)(2,1)S(1)}, bf16[80,384]{1,0:T(8,128)(2,1)S(1)}, u32[]{:S(2)}, u32[]{:S(2)}) collective-permute-start(bf16[80,384]{1,0:T(8,128)(2,1)S(1)} %get-tuple-element.82), channel_id=1, source_target_pairs={{0,3},{1,0},{2,1},{3,2},{4,7},{5,4},{6,5},{7,6},{8,11},{9,8},{10,9... | collective-permute-start | bytes 184328 | tf_op jit(solution)/shard_map/ppermute | solution.py:265
  100.2 4.5 %collective-permute-done.12.a2 = bf16[5,64,384]{2,1,0:T(8,128)(2,1)S(1)} collective-permute-done((bf16[5,64,384]{2,1,0:T(8,128)(2,1)S(1)}, bf16[5,64,384]{2,1,0:T(8,128)(2,1)S(1)}, u32[]{:S(2)}, u32[]{:S(2)}) %collective-permute-start.12) | collective-permute-done | bytes 245792 | tf_op jit(solution)/shard_map/ppermute | solution.py:265
  104.7 1.7 %unpack_y.1 = bf16[3,64,1440]{2,1,0:T(8,128)(2,1)} custom-call(s32[2]{0:T(128)S(1)} %pad_add_fusion.idx, bf16[5,64,384]{2,1,0:T(8,128)(2,1)S(1)} %get-tuple-element.76.a0, bf16[5,64,384]{2,1,0:T(8,128)(2,1)S(1)} %collective-permute-done.11.a1, bf16[5,64,384]{2,1,0:T(8,128)(2,1)S(1)} %collective-permute-done.12.a2, ...), custom_call_target="tpu_custom_call" | custom-call | bytes 1000000 | tf_op jit(solution)/shard_map/unpack_y/pallas_call | solution.py:337
  106.3 1.9 %collective-permute-done.8.b1 = bf16[80,384]{1,0:T(8,128)(2,1)S(1)} collective-permute-done((bf16[80,384]{1,0:T(8,128)(2,1)S(1)}, bf16[80,384]{1,0:T(8,128)(2,1)S(1)}, u32[]{:S(2)}, u32[]{:S(2)}) %collective-permute-start.8) | collective-permute-done | bytes 61472 | tf_op jit(solution)/shard_map/ppermute | solution.py:265
  108.2 1.8 %collective-permute-done.9.b2 = bf16[80,384]{1,0:T(8,128)(2,1)S(1)} collective-permute-done((bf16[80,384]{1,0:T(8,128)(2,1)S(1)}, bf16[80,384]{1,0:T(8,128)(2,1)S(1)}, u32[]{:S(2)}, u32[]{:S(2)}) %collective-permute-start.9) | collective-permute-done | bytes 61472 | tf_op jit(solution)/shard_map/ppermute | solution.py:265
  110.1 1.2 %collective-permute-done.10.b3 = bf16[80,384]{1,0:T(8,128)(2,1)S(1)} collective-permute-done((bf16[80,384]{1,0:T(8,128)(2,1)S(1)}, bf16[80,384]{1,0:T(8,128)(2,1)S(1)}, u32[]{:S(2)}, u32[]{:S(2)}) %collective-permute-start.10) | collective-permute-done | bytes 61472 | tf_op jit(solution)/shard_map/ppermute | solution.py:265
  111.3 1.6 %unpack_g.1 = (bf16[3,64,1440]{2,1,0:T(8,128)(2,1)}, f32[9,4,64]{2,1,0:T(4,128)}) custom-call(s32[2]{0:T(128)S(1)} %pad_add_fusion.idx, bf16[5,64,384]{2,1,0:T(8,128)(2,1)S(1)} %get-tuple-element.76.a0, bf16[5,64,384]{2,1,0:T(8,128)(2,1)S(1)} %collective-permute-done.11.a1, bf16[5,64,384]{2,1,0:T(8,128)(2,1)S(1)} %collective-permute-done.12.a2, ...), custom_call_target="tpu_custom_call" | custom-call | bytes 1000000 | tf_op jit(solution)/shard_map/unpack_g/pallas_call | solution.py:341
  (20 shorter events, 0.1 us)
Async XLA Ops:
  0.6 14.8 %copy-start.4 = (s32[3,5]{1,0:T(4,128)S(1)}, s32[3,5]{1,0:T(4,128)}, u32[]{:S(2)}) copy-start(s32[3,5]{1,0:T(4,128)} %param.7) | copy-start | bytes 184
  0.7 1.1 copy-start
  1.8 1.1 copy-start.1
  2.9 12.8 %copy-start.3 = (bf16[3,5,9,16]{3,0,2,1:T(4,128)(2,1)S(1)}, bf16[3,5,9,16]{3,0,2,1:T(4,128)(2,1)}, u32[]{:S(2)}) copy-start(bf16[3,5,9,16]{3,0,2,1:T(4,128)(2,1)} %param.8) | copy-start | bytes 12964
  4.0 15.7 %collective-permute-start = (bf16[6,64,384]{2,1,0:T(8,128)(2,1)S(1)}, bf16[6,64,384]{2,1,0:T(8,128)(2,1)S(1)}, u32[]{:S(2)}, u32[]{:S(2)}) collective-permute-start(bf16[6,64,384]{2,1,0:T(8,128)(2,1)S(1)} %get-tuple-element.49), channel_id=1, source_target_pairs={{0,1},{1,2},{2,3},{3,0},{4,5},{5,6},{6,7},{7,4},{8,9},{9,10},{10,1... | collective-permute-start | bytes 884744 | tf_op jit(solution)/shard_map/ppermute | solution.py:265
  7.9 22.3 %collective-permute-start.1 = (bf16[6,64,384]{2,1,0:T(8,128)(2,1)S(1)}, bf16[6,64,384]{2,1,0:T(8,128)(2,1)S(1)}, u32[]{:S(2)}, u32[]{:S(2)}) collective-permute-start(bf16[6,64,384]{2,1,0:T(8,128)(2,1)S(1)} %get-tuple-element.50), channel_id=1, source_target_pairs={{0,2},{1,3},{2,0},{3,1},{4,6},{5,7},{6,4},{7,5},{8,10},{9,11},{10,... | collective-permute-start | bytes 884744 | tf_op jit(solution)/shard_map/ppermute | solution.py:265
  13.1 27.1 %collective-permute-start.2 = (bf16[6,64,384]{2,1,0:T(8,128)(2,1)S(1)}, bf16[6,64,384]{2,1,0:T(8,128)(2,1)S(1)}, u32[]{:S(2)}, u32[]{:S(2)}) collective-permute-start(bf16[6,64,384]{2,1,0:T(8,128)(2,1)S(1)} %get-tuple-element.51), channel_id=1, source_target_pairs={{0,3},{1,0},{2,1},{3,2},{4,7},{5,4},{6,5},{7,6},{8,11},{9,8},{10,9... | collective-permute-start | bytes 884744 | tf_op jit(solution)/shard_map/ppermute | solution.py:265
  16.1 28.6 %copy-start.2 = (bf16[9,256,256]{2,1,0:T(8,128)(2,1)S(1)}, bf16[9,256,256]{2,1,0:T(8,128)(2,1)}, u32[]{:S(2)}) copy-start(bf16[9,256,256]{2,1,0:T(8,128)(2,1)} %param.9) | copy-start | bytes 3538948
  41.0 13.1 %collective-permute-start.3 = (bf16[2,400,256]{2,1,0:T(8,128)(2,1)S(1)}, bf16[2,400,256]{2,1,0:T(8,128)(2,1)S(1)}, u32[]{:S(2)}, u32[]{:S(2)}) collective-permute-start(bf16[2,400,256]{2,1,0:T(8,128)(2,1)S(1)} %get-tuple-element.59), channel_id=1, source_target_pairs={{0,4},{4,0},{8,12},{12,8},{16,20},{20,16},{24,28},{28,24},{32,36},... | collective-permute-start | bytes 1228808 | tf_op jit(solution)/shard_map/ppermute | solution.py:293
  41.6 12.6 %collective-permute-start.4 = (bf16[2,400,256]{2,1,0:T(8,128)(2,1)S(1)}, bf16[2,400,256]{2,1,0:T(8,128)(2,1)S(1)}, u32[]{:S(2)}, u32[]{:S(2)}) collective-permute-start(bf16[2,400,256]{2,1,0:T(8,128)(2,1)S(1)} %get-tuple-element.60), channel_id=1, source_target_pairs={{4,8},{8,4},{12,16},{16,12},{20,24},{24,20},{28,32},{32,28},{36,40... | collective-permute-start | bytes 1228808 | tf_op jit(solution)/shard_map/ppermute | solution.py:292
  50.4 10.9 %collective-permute-start.5 = (bf16[2,384,256]{2,1,0:T(8,128)(2,1)S(1)}, bf16[2,384,256]{2,1,0:T(8,128)(2,1)S(1)}, u32[]{:S(2)}, u32[]{:S(2)}) collective-permute-start(bf16[2,384,256]{2,1,0:T(8,128)(2,1)S(1)} %get-tuple-element.69), channel_id=1, source_target_pairs={{0,4},{4,0},{8,12},{12,8},{16,20},{20,16},{24,28},{28,24},{32,36},... | collective-permute-start | bytes 1179656 | tf_op jit(solution)/shard_map/ppermute | solution.py:311
  50.5 10.8 %collective-permute-start.6 = (bf16[2,384,256]{2,1,0:T(8,128)(2,1)S(1)}, bf16[2,384,256]{2,1,0:T(8,128)(2,1)S(1)}, u32[]{:S(2)}, u32[]{:S(2)}) collective-permute-start(bf16[2,384,256]{2,1,0:T(8,128)(2,1)S(1)} %get-tuple-element.70), channel_id=1, source_target_pairs={{4,8},{8,4},{12,16},{16,12},{20,24},{24,20},{28,32},{32,28},{36,40... | collective-permute-start | bytes 1179656 | tf_op jit(solution)/shard_map/ppermute | solution.py:310
  61.4 2.2 %collective-permute-start.7 = (bf16[1280,256]{1,0:T(8,128)(2,1)S(1)}, bf16[1280,256]{1,0:T(8,128)(2,1)S(1)}, u32[]{:S(2)}, u32[]{:S(2)}) collective-permute-start(bf16[1280,256]{1,0:T(8,128)(2,1)S(1)} %get-tuple-element.71), channel_id=1, source_target_pairs={{0,4},{4,0},{8,12},{12,8},{16,20},{20,16},{24,28},{28,24},{32,36},... | collective-permute-start | bytes 1966088 | tf_op jit(solution)/shard_map/ppermute | solution.py:325
  65.1 21.9 %all-to-all-start = ((bf16[32,40,256]{2,1,0:T(8,128)(2,1)}), bf16[32,40,256]{2,1,0:T(8,128)(2,1)S(1)}, u32[]{:S(2)}, u32[]{:S(2)}) async-start(bf16[32,40,256]{2,1,0:T(8,128)(2,1)} %bitcast.5), calls=%async_computation | async-start | bytes 1310720 | tf_op jit(solution)/shard_map/all_to_all | solution.py:335
  74.8 21.9 %collective-permute-start.11 = (bf16[5,64,384]{2,1,0:T(8,128)(2,1)S(1)}, bf16[5,64,384]{2,1,0:T(8,128)(2,1)S(1)}, u32[]{:S(2)}, u32[]{:S(2)}) collective-permute-start(bf16[5,64,384]{2,1,0:T(8,128)(2,1)S(1)} %get-tuple-element.83), channel_id=1, source_target_pairs={{0,1},{1,2},{2,3},{3,0},{4,5},{5,6},{6,7},{7,4},{8,9},{9,10},{10,1... | collective-permute-start | bytes 737288 | tf_op jit(solution)/shard_map/ppermute | solution.py:265
  76.3 28.4 %collective-permute-start.12 = (bf16[5,64,384]{2,1,0:T(8,128)(2,1)S(1)}, bf16[5,64,384]{2,1,0:T(8,128)(2,1)S(1)}, u32[]{:S(2)}, u32[]{:S(2)}) collective-permute-start(bf16[5,64,384]{2,1,0:T(8,128)(2,1)S(1)} %get-tuple-element.84), channel_id=1, source_target_pairs={{0,2},{1,3},{2,0},{3,1},{4,6},{5,7},{6,4},{7,5},{8,10},{9,11},{10,... | collective-permute-start | bytes 737288 | tf_op jit(solution)/shard_map/ppermute | solution.py:265
  80.4 24.3 %collective-permute-start.13 = (bf16[5,64,384]{2,1,0:T(8,128)(2,1)S(1)}, bf16[5,64,384]{2,1,0:T(8,128)(2,1)S(1)}, u32[]{:S(2)}, u32[]{:S(2)}) collective-permute-start(bf16[5,64,384]{2,1,0:T(8,128)(2,1)S(1)} %get-tuple-element.85), channel_id=1, source_target_pairs={{0,3},{1,0},{2,1},{3,2},{4,7},{5,4},{6,5},{7,6},{8,11},{9,8},{10,9... | collective-permute-start | bytes 737288 | tf_op jit(solution)/shard_map/ppermute | solution.py:265
  87.7 20.5 %collective-permute-start.8 = (bf16[80,384]{1,0:T(8,128)(2,1)S(1)}, bf16[80,384]{1,0:T(8,128)(2,1)S(1)}, u32[]{:S(2)}, u32[]{:S(2)}) collective-permute-start(bf16[80,384]{1,0:T(8,128)(2,1)S(1)} %get-tuple-element.80), channel_id=1, source_target_pairs={{0,1},{1,2},{2,3},{3,0},{4,5},{5,6},{6,7},{7,4},{8,9},{9,10},{10,1... | collective-permute-start | bytes 184328 | tf_op jit(solution)/shard_map/ppermute | solution.py:265
  89.1 21.0 %collective-permute-start.9 = (bf16[80,384]{1,0:T(8,128)(2,1)S(1)}, bf16[80,384]{1,0:T(8,128)(2,1)S(1)}, u32[]{:S(2)}, u32[]{:S(2)}) collective-permute-start(bf16[80,384]{1,0:T(8,128)(2,1)S(1)} %get-tuple-element.81), channel_id=1, source_target_pairs={{0,2},{1,3},{2,0},{3,1},{4,6},{5,7},{6,4},{7,5},{8,10},{9,11},{10,... | collective-permute-start | bytes 184328 | tf_op jit(solution)/shard_map/ppermute | solution.py:265
  96.7 14.6 %collective-permute-start.10 = (bf16[80,384]{1,0:T(8,128)(2,1)S(1)}, bf16[80,384]{1,0:T(8,128)(2,1)S(1)}, u32[]{:S(2)}, u32[]{:S(2)}) collective-permute-start(bf16[80,384]{1,0:T(8,128)(2,1)S(1)} %get-tuple-element.82), channel_id=1, source_target_pairs={{0,3},{1,0},{2,1},{3,2},{4,7},{5,4},{6,5},{7,6},{8,11},{9,8},{10,9... | collective-permute-start | bytes 184328 | tf_op jit(solution)/shard_map/ppermute | solution.py:265
